TPU v7x, 1024 devices: a whole 8x8x8 slice. The times are simulated.
1024 devices in a mesh: grp: 64 (over y, x), loc: 16 (over z, core).
Axes of the slice: x: 8, y: 8, z: 8, core: 2. Of those that a mesh axis runs over, the one named last changes fastest.
Arguments:
- token_grads: bfloat16 [131072, 2048], P(('grp', 'loc')), may hold values from -6 to 6
- owner_loc: int32 [131072, 2], P(('grp', 'loc')), may hold values from 0 to 15, as said below
- owner_group: int32 [131072, 2], P(('grp', 'loc')), may hold values from 0 to 63, as said below
- owner_row: int32 [131072, 2], P(('grp', 'loc')), may hold values from 0 to 31, as said below
- embed_table: float32 [32768, 2048], P(('grp', 'loc')), may hold values from -6 to 6
- first_moment: float32 [32768, 2048], P(('grp', 'loc')), may hold values from -4 to 4
- second_moment: float32 [32768, 2048], P(('grp', 'loc')), may hold values from 0.01 to 1
Outputs:
- new_table: float32 [32768, 2048], P(('grp', 'loc'))
- new_first: float32 [32768, 2048], P(('grp', 'loc'))
- new_second: float32 [32768, 2048], P(('grp', 'loc'))
Inputs may be any that keep to these rules, and one draw needn't show every extreme that they name: `owner_loc`: among the 256 entries of one device, no value appears more than 32 times, and one value appears exactly 32 times. Among all entries held by the devices of one grp index that share one owner_loc value, no owner_group value appears more than 8 times, and one appears exactly 8 times. Among all entries held by the devices of one grp index that share one owner_loc value and one owner_group value, at most 4 distinct owner_row values appear, and exactly 4 in some.
All inputs are finite; a program needn't handle non-finite values.
Results may differ from a plain program's by a relative error of at most 0.0029.
Values may be sent and summed in bfloat16 or wider, within the bound.
No kernel may reach another device: no remote copies, remote signals or barrier semaphores. Data moves between devices by JAX's collectives and lax.ppermute only.
A program may use at most 32 MiB of HBM per device.

v0:
```python
import jax
import jax.numpy as jnp
from jax import lax
from jax.sharding import PartitionSpec as P

ADAM_STEP = 100


beta_one = 0.9
beta_two = 0.999
learn_rate = 0.01
epsilon = 1e-08


def adam_rows(embed_table, first_moment, second_moment, row_grad, touched):
    corr_one = 1.0 - beta_one**ADAM_STEP
    corr_two = 1.0 - beta_two**ADAM_STEP
    first_next = beta_one * first_moment + (1.0 - beta_one) * row_grad
    second_next = beta_two * second_moment + (1.0 - beta_two) * row_grad * row_grad
    update = learn_rate * (first_next / corr_one) / (jnp.sqrt(second_next / corr_two) + epsilon)
    table_next = embed_table - update
    mask = touched[:, None]
    return (
        jnp.where(mask, table_next, embed_table),
        jnp.where(mask, first_next, first_moment),
        jnp.where(mask, second_next, second_moment),
    )


def exclusive_rank(target, bucket_count):
    member = (target[:, None] == jnp.arange(bucket_count, dtype=jnp.int32)[None, :]).astype(
        jnp.int32
    )
    before = jnp.cumsum(member, axis=0) - member
    return jnp.sum(before * member, axis=1)


def per_device(
    token_grads, owner_loc, owner_group, owner_row, embed_table, first_moment, second_moment
):
    loc_count = lax.axis_size("loc")
    grp_count = lax.axis_size("grp")
    token_count = token_grads.shape[0]
    feature_width = token_grads.shape[1]
    rows_owned = embed_table.shape[0]
    entries = 2 * token_count
    cap_loc = 4 * token_count // loc_count
    cap_raw = max(4, 4 * token_count // grp_count)
    slots_one = loc_count * cap_loc
    row_index = jnp.arange(rows_owned, dtype=jnp.int32)
    dest_loc = owner_loc.reshape(entries)
    row_tag = (owner_group * rows_owned + owner_row).reshape(entries)
    slot_one = dest_loc * cap_loc + exclusive_rank(dest_loc, loc_count)
    tag_one = jnp.full((slots_one,), -1, jnp.int32).at[slot_one].set(row_tag)
    select = slot_one[None, :] == jnp.arange(slots_one, dtype=jnp.int32)[:, None]
    select = jnp.sum(select.reshape(slots_one, token_count, 2).astype(jnp.int32), axis=2).astype(
        jnp.bfloat16
    )
    packed_one = jnp.dot(select, token_grads, preferred_element_type=jnp.float32).astype(
        jnp.bfloat16
    )
    arrived, arrived_tag = (
        lax.all_to_all(
            packed_one.reshape(loc_count, cap_loc, feature_width),
            "loc",
            split_axis=0,
            concat_axis=0,
            tiled=True,
        ),
        lax.all_to_all(
            tag_one.reshape(loc_count, cap_loc), "loc", split_axis=0, concat_axis=0, tiled=True
        ),
    )
    arrived = arrived.reshape(slots_one, feature_width)
    arrived_tag = arrived_tag.reshape(slots_one)
    valid = arrived_tag >= 0
    slots_two = grp_count * cap_raw
    dest_group = jnp.where(valid, arrived_tag // rows_owned, grp_count)
    slot_two = jnp.where(
        valid, dest_group * cap_raw + exclusive_rank(dest_group, grp_count), slots_two
    )
    tag_two = (
        jnp.full((slots_two + 1,), -1, jnp.int32)
        .at[slot_two]
        .set(arrived_tag % rows_owned)[:slots_two]
    )
    select_two = (slot_two[None, :] == jnp.arange(slots_two, dtype=jnp.int32)[:, None]).astype(
        jnp.bfloat16
    )
    packed_two = jnp.dot(select_two, arrived, preferred_element_type=jnp.float32).astype(
        jnp.bfloat16
    )
    landed, landed_row = (
        lax.all_to_all(
            packed_two.reshape(grp_count, cap_raw, feature_width),
            "grp",
            split_axis=0,
            concat_axis=0,
            tiled=True,
        ),
        lax.all_to_all(
            tag_two.reshape(grp_count, cap_raw), "grp", split_axis=0, concat_axis=0, tiled=True
        ),
    )
    member = landed_row[:, None, :] == row_index[None, :, None]
    block_sums = jnp.einsum(
        "grs,gsd->grd", member.astype(jnp.bfloat16), landed, preferred_element_type=jnp.float32
    ).astype(jnp.bfloat16)
    row_grad = jnp.sum(block_sums, axis=0, dtype=jnp.float32)
    touched = jnp.sum(member.astype(jnp.int32), axis=(0, 2)) > 0
    new_table, new_first, new_second = adam_rows(
        embed_table, first_moment, second_moment, row_grad, touched
    )
    return (new_table, new_first, new_second)


def solution(mesh):
    return jax.shard_map(
        per_device,
        mesh=mesh,
        in_specs=(
            P(("grp", "loc"), None),
            P(("grp", "loc"), None),
            P(("grp", "loc"), None),
            P(("grp", "loc"), None),
            P(("grp", "loc"), None),
            P(("grp", "loc"), None),
            P(("grp", "loc"), None),
        ),
        out_specs=(P(("grp", "loc"), None), P(("grp", "loc"), None), P(("grp", "loc"), None)),
        check_vma=False,
    )
```

profile of v0, /device:TPU:34, one launch (start us, length us, event | category | flops | bytes accessed | tf_op | source)
XLA Modules:
  0.0 173.9 jit_solution(8411436587249598879)
XLA Ops:
  0.6 0.8 copy.39
  1.8 0.6 reduce-window.14
  2.9 0.7 broadcast_multiply_fusion
  3.9 0.7 multiply_add_fusion.1
  4.8 1.4 scatter_custom_fusion
  6.2 0.7 all_to_all.18
  6.9 16.8 %all-to-all-start = ((s32[16,1,32]{2,1,0:T(1,128)}), s32[16,1,32]{2,1,0:T(1,128)S(1)}, u32[]{:S(2)}, u32[]{:S(2)}) async-start(s32[16,1,32]{2,1,0:T(1,128)} %all_to_all.18), calls=%async_computation | async-start | bytes 16384 | tf_op jit(solution)/shard_map/all_to_all | solution.py:70
  23.8 2.0 %convolution_convert_fusion = bf16[512,2048]{1,0:T(8,128)(2,1)} fusion(bf16[128,2048]{1,0:T(8,128)(2,1)S(1)} %copy-done, s32[512,128]{1,0:T(8,128)S(1)} %convert_reduce_fusion.1), kind=kOutput, calls=%fused_computation.3 | convolution fusion | flops 269549568 | bytes 2883584 | tf_op jit(solution)/shard_map/dot_general | solution.py:59
  25.8 5.4 %all-to-all-done = s32[16,1,32]{2,1,0:T(1,128)S(1)} async-done(((s32[16,1,32]{2,1,0:T(1,128)}), s32[16,1,32]{2,1,0:T(1,128)S(1)}, u32[]{:S(2)}, u32[]{:S(2)}) %all-to-all-start) | async-done | bytes 2080 | tf_op jit(solution)/shard_map/all_to_all | solution.py:70
  31.2 3.7 %all-to-all-start.2 = ((bf16[16,32,2048]{2,1,0:T(8,128)(2,1)}), bf16[16,32,2048]{2,1,0:T(8,128)(2,1)S(1)}, u32[]{:S(2)}, u32[]{:S(2)}) async-start(bf16[16,32,2048]{2,1,0:T(8,128)(2,1)} %bitcast.8), calls=%async_computation.2 | async-start | bytes 4194304 | tf_op jit(solution)/shard_map/all_to_all | solution.py:63
  35.1 1.2 reduce-window.16
  36.3 0.2 slice_reduce_fusion
  36.6 0.5 broadcast.283
  37.1 0.7 reduce.11
  38.0 2.4 %scatter_custom_fusion.1 = s32[513]{0:T(1024)S(1)} fusion(s32[512]{0:T(512)S(1)} %bitcast.59, s32[512]{0:T(512)S(1)} %get-tuple-element.6, s32[]{:T(128)} %constant.26.clone.1), kind=kCustom, calls=%fused_computation.63 | custom fusion | bytes 2056 | tf_op jit(solution)/shard_map/scatter | solution.py:85
  40.5 0.7 all_to_all.20
  41.2 42.9 %all-to-all-done.2 = bf16[16,32,2048]{2,1,0:T(8,128)(2,1)S(1)} async-done(((bf16[16,32,2048]{2,1,0:T(8,128)(2,1)}), bf16[16,32,2048]{2,1,0:T(8,128)(2,1)S(1)}, u32[]{:S(2)}, u32[]{:S(2)}) %all-to-all-start.2) | async-done | bytes 2097184 | tf_op jit(solution)/shard_map/all_to_all | solution.py:63
  84.1 13.1 %all-to-all-start.1 = ((s32[64,1,8]{2,1,0:T(1,128)}), s32[64,1,8]{2,1,0:T(1,128)S(1)}, u32[]{:S(2)}, u32[]{:S(2)}) async-start(s32[64,1,8]{2,1,0:T(1,128)} %bitcast.6), calls=%async_computation.1 | async-start | bytes 65536 | tf_op jit(solution)/shard_map/all_to_all | solution.py:101
  97.2 2.6 %fusion = bf16[64,8,2048]{2,1,0:T(8,128)(2,1)} fusion(bf16[512,2048]{1,0:T(8,128)(2,1)S(1)} %bitcast.52, s32[512]{0:T(512)S(1)} %add_select_fusion.3), kind=kOutput, calls=%fused_computation.5 | convolution fusion | flops 1075052544 | bytes 4196352 | tf_op jit(solution)/shard_map/dot_general | solution.py:90
  99.8 6.6 %all-to-all-done.1 = s32[64,1,8]{2,1,0:T(1,128)S(1)} async-done(((s32[64,1,8]{2,1,0:T(1,128)}), s32[64,1,8]{2,1,0:T(1,128)S(1)}, u32[]{:S(2)}, u32[]{:S(2)}) %all-to-all-start.1) | async-done | bytes 2080 | tf_op jit(solution)/shard_map/all_to_all | solution.py:101
  106.5 7.3 %all-to-all-start.3 = ((bf16[64,8,2048]{2,1,0:T(8,128)(2,1)}), bf16[64,8,2048]{2,1,0:T(8,128)(2,1)S(1)}, u32[]{:S(2)}, u32[]{:S(2)}) async-start(bf16[64,8,2048]{2,1,0:T(8,128)(2,1)} %fusion), calls=%async_computation.3 | async-start | bytes 4194304 | tf_op jit(solution)/shard_map/all_to_all | solution.py:94
  114.0 51.8 %all-to-all-done.3 = bf16[64,8,2048]{2,1,0:T(8,128)(2,1)S(1)} async-done(((bf16[64,8,2048]{2,1,0:T(8,128)(2,1)}), bf16[64,8,2048]{2,1,0:T(8,128)(2,1)S(1)}, u32[]{:S(2)}, u32[]{:S(2)}) %all-to-all-start.3) | async-done | bytes 2097184 | tf_op jit(solution)/shard_map/all_to_all | solution.py:94
  165.8 6.9 %convert_reduce_fusion = f32[32,2048]{1,0:T(8,128)S(1)} fusion(bf16[64,8,2048]{2,1,0:T(8,128)(2,1)S(1)} %all-to-all-done.3, s32[64,8]{1,0:T(8,128)S(1)} %bitcast.54), kind=kOutput, calls=%fused_computation.2 | convolution fusion | flops 79642624 | bytes 2361344 | tf_op jit(solution)/shard_map/grs,gsd->grd/dot_general | solution.py:106
  172.8 1.1 fusion.4
  (37 shorter events, 2.0 us)
Async XLA Ops:
  0.6 23.2 %copy-start = (bf16[128,2048]{1,0:T(8,128)(2,1)S(1)}, bf16[128,2048]{1,0:T(8,128)(2,1)}, u32[]{:S(2)}) copy-start(bf16[128,2048]{1,0:T(8,128)(2,1)} %param.7) | copy-start | bytes 1572868
  6.9 24.3 %all-to-all-start = ((s32[16,1,32]{2,1,0:T(1,128)}), s32[16,1,32]{2,1,0:T(1,128)S(1)}, u32[]{:S(2)}, u32[]{:S(2)}) async-start(s32[16,1,32]{2,1,0:T(1,128)} %all_to_all.18), calls=%async_computation | async-start | bytes 16384 | tf_op jit(solution)/shard_map/all_to_all | solution.py:70
  31.2 52.9 %all-to-all-start.2 = ((bf16[16,32,2048]{2,1,0:T(8,128)(2,1)}), bf16[16,32,2048]{2,1,0:T(8,128)(2,1)S(1)}, u32[]{:S(2)}, u32[]{:S(2)}) async-start(bf16[16,32,2048]{2,1,0:T(8,128)(2,1)} %bitcast.8), calls=%async_computation.2 | async-start | bytes 4194304 | tf_op jit(solution)/shard_map/all_to_all | solution.py:63
  84.1 22.4 %all-to-all-start.1 = ((s32[64,1,8]{2,1,0:T(1,128)}), s32[64,1,8]{2,1,0:T(1,128)S(1)}, u32[]{:S(2)}, u32[]{:S(2)}) async-start(s32[64,1,8]{2,1,0:T(1,128)} %bitcast.6), calls=%async_computation.1 | async-start | bytes 65536 | tf_op jit(solution)/shard_map/all_to_all | solution.py:101
  106.5 59.3 %all-to-all-start.3 = ((bf16[64,8,2048]{2,1,0:T(8,128)(2,1)}), bf16[64,8,2048]{2,1,0:T(8,128)(2,1)S(1)}, u32[]{:S(2)}, u32[]{:S(2)}) async-start(bf16[64,8,2048]{2,1,0:T(8,128)(2,1)} %fusion), calls=%async_computation.3 | async-start | bytes 4194304 | tf_op jit(solution)/shard_map/all_to_all | solution.py:94
  113.8 58.9 %copy-start.1 = (f32[32,2048]{1,0:T(8,128)S(1)}, f32[32,2048]{1,0:T(8,128)}, u32[]{:S(2)}) copy-start(f32[32,2048]{1,0:T(8,128)} %param.13) | copy-start | bytes 786436
  113.9 58.9 %copy-start.2 = (f32[32,2048]{1,0:T(8,128)S(1)}, f32[32,2048]{1,0:T(8,128)}, u32[]{:S(2)}) copy-start(f32[32,2048]{1,0:T(8,128)} %param.11) | copy-start | bytes 786436
  113.9 58.9 %copy-start.3 = (f32[32,2048]{1,0:T(8,128)S(1)}, f32[32,2048]{1,0:T(8,128)}, u32[]{:S(2)}) copy-start(f32[32,2048]{1,0:T(8,128)} %param.12) | copy-start | bytes 786436
where the time goes:
time: 175 us; the launch traced here: 174 us
  waiting for transfers between devices  107 us (61%)
  starting transfers between devices  41 us (23%)
  matrix products  11.6 us (7%)
  local copies, waits for them, and re-layouts  8.27 us (5%)
  other arithmetic  5.59 us (3%)
    all_to_all x1, waiting for transfers between devices, per_device(): lax.all_to_all(packed_two.reshape(grp_count, cap_raw, feature_width), 'gr...  51.8 us
    all_to_all x1, waiting for transfers between devices, per_device(): lax.all_to_all(packed_one.reshape(loc_count, cap_loc, feature_width), 'lo...  42.9 us
    all_to_all x1, starting transfers between devices, per_device(): lax.all_to_all(tag_one.reshape(loc_count, cap_loc), 'loc', split_axis=0,...  16.8 us
    all_to_all x1, starting transfers between devices, per_device(): lax.all_to_all(tag_two.reshape(grp_count, cap_raw), 'grp', split_axis=0,...  13.1 us
    all_to_all x1, starting transfers between devices, per_device(): lax.all_to_all(packed_two.reshape(grp_count, cap_raw, feature_width), 'gr...  7.35 us
    dot_general x1, matrix products, per_device(): jnp.einsum('grs,gsd->grd', member.astype(jnp.bfloat16), landed, preferred...  6.93 us
    all_to_all x1, waiting for transfers between devices, per_device(): lax.all_to_all(tag_two.reshape(grp_count, cap_raw), 'grp', split_axis=0,...  6.64 us
    all_to_all x1, waiting for transfers between devices, per_device(): lax.all_to_all(tag_one.reshape(loc_count, cap_loc), 'loc', split_axis=0,...  5.37 us
  transfers between devices with their start and end apart: 4, of which 4 were waited for; matrix products, arithmetic and copies ran while one was open for 6% of the time, Pallas kernels for 0%

commit v1 on v0

v1 whole, which is shorter than its diff:
```python
import functools

import jax
import jax.numpy as jnp
from jax import lax
from jax.experimental import pallas as pl
from jax.experimental.pallas import tpu as pltpu
from jax.sharding import PartitionSpec as P

ADAM_STEP = 100
SLOTS = 4

beta_one = 0.9
beta_two = 0.999
learn_rate = 0.01
epsilon = 1e-08


def iota(shape, dim):
    return lax.broadcasted_iota(jnp.int32, shape, dim)


def plan_kernel(groups, locs, rows, me_ref, ids_ref, select_ref, tag_ref):
    me = me_ref[0]
    slots = groups * SLOTS
    ids = ids_ref[...]
    tokens = ids.shape[1]
    row = ids % rows
    owner = ids // rows
    group = jnp.where(owner % locs == me, owner // locs, -1)
    present = jnp.zeros((groups, rows), jnp.float32)
    for i in range(ids.shape[0]):
        in_group = jnp.where(group[i : i + 1] == iota((groups, tokens), 0), 1.0, 0.0)
        in_row = jnp.where(row[i : i + 1] == iota((rows, tokens), 0), 1.0, 0.0)
        present += lax.dot_general(
            in_group.astype(jnp.bfloat16),
            in_row.astype(jnp.bfloat16),
            (((1,), (1,)), ((), ())),
            preferred_element_type=jnp.float32,
        )
    hit = jnp.where(present > 0.5, 1.0, 0.0).astype(jnp.bfloat16)
    below = jnp.where(iota((rows, rows), 0) < iota((rows, rows), 1), 1.0, 0.0).astype(jnp.bfloat16)
    spread = jnp.where(iota((slots, groups), 0) // SLOTS == iota((slots, groups), 1), 1.0, 0.0)
    hits = jnp.dot(spread.astype(jnp.bfloat16), hit, preferred_element_type=jnp.float32)
    rank = jnp.dot(hits.astype(jnp.bfloat16), below, preferred_element_type=jnp.float32)
    turn = (iota((slots, rows), 0) % SLOTS).astype(jnp.float32)
    mine = (hits > 0.5) & (jnp.abs(rank - turn) < 0.5)
    lane = iota((slots, rows), 1)
    slot_row = jnp.max(jnp.where(mine, lane, -1), axis=1, keepdims=True)
    slot_group = iota((slots, 1), 0) // SLOTS
    slot_id = jnp.where(slot_row >= 0, (slot_group * locs + me) * rows + slot_row, -1)
    for i in range(locs):
        one = jnp.where(ids[2 * i : 2 * i + 1] == slot_id, 1.0, 0.0)
        two = jnp.where(ids[2 * i + 1 : 2 * i + 2] == slot_id, 1.0, 0.0)
        select_ref[:, i * tokens : (i + 1) * tokens] = (one + two).astype(jnp.bfloat16)
    spot = iota((slots, 128), 1)
    placed = jnp.where(
        (spot % SLOTS == iota((slots, 128), 0) % SLOTS) & (spot < 2 * SLOTS), slot_row.astype(jnp.float32), 0.0
    )
    tag = lax.dot_general(
        spread.astype(jnp.bfloat16),
        placed.astype(jnp.bfloat16),
        (((0,), (0,)), ((), ())),
        preferred_element_type=jnp.float32,
    )
    tag_ref[...] = tag.astype(jnp.int32)


def member_kernel(rows, tag_ref, member_ref):
    groups = tag_ref.shape[0]
    wide = groups * 2 * SLOTS
    tag = tag_ref[...].astype(jnp.float32).astype(jnp.bfloat16)
    spread = jnp.where(iota((groups, wide), 1) // (2 * SLOTS) == iota((groups, wide), 0), 1.0, 0.0)
    lanes = lax.dot_general(
        tag,
        spread.astype(jnp.bfloat16),
        (((0,), (0,)), ((), ())),
        preferred_element_type=jnp.float32,
    )[: 2 * SLOTS]
    spot = iota((2 * SLOTS, wide), 1) % (2 * SLOTS)
    line = jnp.sum(jnp.where(iota((2 * SLOTS, wide), 0) == spot, lanes, 0.0), axis=0, keepdims=True)
    same = line.astype(jnp.int32) == iota((rows, wide), 0)
    half = iota((rows, wide), 1) // SLOTS % 2
    for h in range(2):
        member_ref[h] = jnp.where(same & (half == h), 1.0, 0.0).astype(jnp.bfloat16)


def combine_kernel(select_ref, low_ref, high_ref, out_ref):
    select = select_ref[...]
    low = jnp.dot(select, low_ref[...], preferred_element_type=jnp.float32)
    high = jnp.dot(select, high_ref[...], preferred_element_type=jnp.float32)
    slots, width = low.shape
    top = iota((slots, width), 0) % 8 < SLOTS
    even = jnp.where(top, low, pltpu.roll(high, SLOTS, 0))
    odd = jnp.where(top, pltpu.roll(low, slots - SLOTS, 0), high)
    even = even.reshape(slots // 8, 1, 8, width)
    odd = odd.reshape(slots // 8, 1, 8, width)
    both = jnp.concatenate([even, odd], axis=1).reshape(slots // SLOTS, 8, width)
    out_ref[...] = both.astype(jnp.bfloat16)


def adam_kernel(member_ref, landed_ref, table_ref, first_ref, second_ref, t_out, f_out, s_out):
    member = member_ref[0]
    groups, eight, width = landed_ref.shape
    landed = landed_ref[...].reshape(groups * eight, width)
    grad = jnp.dot(member, landed, preferred_element_type=jnp.float32)
    touched = jnp.sum(member.astype(jnp.float32), axis=1, keepdims=True) > 0.5
    corr_one = 1.0 - beta_one**ADAM_STEP
    corr_two = 1.0 - beta_two**ADAM_STEP
    first, second, table = first_ref[...], second_ref[...], table_ref[...]
    first_next = beta_one * first + (1.0 - beta_one) * grad
    second_next = beta_two * second + (1.0 - beta_two) * grad * grad
    update = learn_rate * (first_next / corr_one) / (jnp.sqrt(second_next / corr_two) + epsilon)
    t_out[...] = jnp.where(touched, table - update, table)
    f_out[...] = jnp.where(touched, first_next, first)
    s_out[...] = jnp.where(touched, second_next, second)


VMEM = pl.BlockSpec(memory_space=pltpu.VMEM)


def make_plan(me, ids, groups, locs, rows):
    tokens = ids.shape[1]
    return pl.pallas_call(
        functools.partial(plan_kernel, groups, locs, rows),
        out_shape=(
            jax.ShapeDtypeStruct((groups * SLOTS, locs * tokens), jnp.bfloat16),
            jax.ShapeDtypeStruct((groups, 128), jnp.int32),
        ),
        in_specs=[pl.BlockSpec(memory_space=pltpu.SMEM), VMEM],
        out_specs=(VMEM, VMEM),
        cost_estimate=pl.CostEstimate(flops=20_000_000, bytes_accessed=2_000_000, transcendentals=0),
        compiler_params=pltpu.CompilerParams(vmem_limit_bytes=32 << 20),
    )(me, ids)


def make_member(tag, rows):
    groups = tag.shape[0]
    return pl.pallas_call(
        functools.partial(member_kernel, rows),
        out_shape=jax.ShapeDtypeStruct((2, rows, groups * 2 * SLOTS), jnp.bfloat16),
        in_specs=[VMEM],
        out_specs=VMEM,
        compiler_params=pltpu.CompilerParams(vmem_limit_bytes=32 << 20),
    )(tag)


def combine(select, grads, groups):
    slots, tokens = select.shape
    width = grads.shape[1]
    half = width // 2
    block = 256
    steps = half // block
    return pl.pallas_call(
        combine_kernel,
        grid=(steps,),
        out_shape=jax.ShapeDtypeStruct((groups, 2 * SLOTS, half), jnp.bfloat16),
        in_specs=[
            pl.BlockSpec((slots, tokens), lambda c: (0, 0)),
            pl.BlockSpec((tokens, block), lambda c: (0, c)),
            pl.BlockSpec((tokens, block), lambda c: (0, c + steps)),
        ],
        out_specs=pl.BlockSpec((groups, 2 * SLOTS, block), lambda c: (0, 0, c)),
        compiler_params=pltpu.CompilerParams(vmem_limit_bytes=58 << 20),
    )(select, grads, grads)


def update(member, landed, table, first, second):
    groups, eight, half = landed.shape
    rows, width = table.shape
    block = 512
    steps = half // block
    state = pl.BlockSpec((rows, block), lambda i: (0, i))
    return pl.pallas_call(
        adam_kernel,
        grid=(2 * steps,),
        out_shape=(jax.ShapeDtypeStruct(table.shape, table.dtype),) * 3,
        in_specs=[
            pl.BlockSpec((1, rows, groups * eight), lambda i: (i // steps, 0, 0)),
            pl.BlockSpec((groups, eight, block), lambda i: (0, 0, i % steps)),
            state,
            state,
            state,
        ],
        out_specs=(state, state, state),
        compiler_params=pltpu.CompilerParams(vmem_limit_bytes=32 << 20),
    )(member, landed, table, first, second)


def per_device(
    token_grads, owner_loc, owner_group, owner_row, embed_table, first_moment, second_moment
):
    locs = lax.axis_size("loc")
    groups = lax.axis_size("grp")
    rows = embed_table.shape[0]
    grads = lax.all_gather(token_grads, "loc", axis=0, tiled=True)
    row_id = ((owner_group * locs + owner_loc) * rows + owner_row).T
    ids = lax.all_gather(row_id, "loc", axis=0, tiled=True)
    me = lax.axis_index("loc").astype(jnp.int32).reshape(1)
    select, tag = make_plan(me, ids, groups, locs, rows)
    came = lax.all_to_all(
        tag.reshape(groups, 1, 128), "grp", split_axis=0, concat_axis=0, tiled=True
    ).reshape(groups, 128)
    member = make_member(came, rows)
    sums = combine(select, grads, groups)
    landed = lax.all_to_all(sums, "grp", split_axis=0, concat_axis=0, tiled=True)
    return tuple(update(member, landed, embed_table, first_moment, second_moment))


def solution(mesh):
    rows = P(("grp", "loc"), None)
    return jax.shard_map(
        per_device, mesh=mesh, in_specs=(rows,) * 7, out_specs=(rows,) * 3, check_vma=False
    )
```

time: 175 us -> 144 us (0.82)
  waiting for transfers between devices: 107 us -> 61.6 us
  blocking collectives: 0 us -> 29.5 us
  starting transfers between devices: 41 us -> 25.8 us
  between operations: 0.83 us -> 14.1 us
  matrix products: 11.6 us -> 0 us
  Pallas kernels: 0 us -> 11.2 us
  local copies, waits for them, and re-layouts: 8.27 us -> 1.07 us
  other arithmetic: 5.59 us -> 0.72 us
    all_to_all x4 -> x2, waiting for transfers between devices: 107 us -> 30.3 us  [the longest x1 30.3 us: per_device(): lax.all_to_all(sums, 'grp', split_axis=0, concat_axis=0, tiled=True)]
    all_gather x0 -> x1, waiting for transfers between devices: none -> 30.6 us  [per_device(): grads = lax.all_gather(token_grads, 'loc', axis=0, tiled=True)]
    all_gather x0 -> x1, blocking collectives: none -> 29.5 us  [per_device(): ids = lax.all_gather(row_id, 'loc', axis=0, tiled=True)]
    all_to_all x4 -> x2, starting transfers between devices: 41 us -> 25.8 us  [the longest x1 13.1 us: per_device(): lax.all_to_all(tag.reshape(groups, 1, 128), 'grp', split_axis=0, concat_a...]
    dot_general x3 -> x0, matrix products: 11.6 us -> none  [the longest x1 6.93 us: per_device(): jnp.einsum('grs,gsd->grd', member.astype(jnp.bfloat16), landed, preferred...]
    pallas_call x0 -> x4, Pallas kernels: none -> 11.2 us  [the longest x1 6.69 us: combine(): pl.pallas_call(combine_kernel, grid=(steps,), out_shape=jax.ShapeDtypeStr...]
    scatter x2 -> x0, local copies, waits for them, and re-layouts: 3.84 us -> none  [the longest x1 2.45 us: per_device(): tag_two = jnp.full((slots_two + 1,), -1, jnp.int32).at[slot_two].set(arri...]
    all_to_all x3 -> x0, local copies, waits for them, and re-layouts: 1.91 us -> none  [the longest x2 1.2 us: per_device(): lax.all_to_all(tag_one.reshape(loc_count, cap_loc), 'loc', split_axis=0,...]
  transfers between devices with their start and end apart: 4 -> 3, of which waited for: 4 -> 2; matrix products, arithmetic and copies ran while one was open for 6% -> 0% of each run, Pallas kernels for 0% -> 6%
where the time goes in v1:
time: 144 us
  waiting for transfers between devices  61.6 us (43%)
  blocking collectives  29.5 us (20%)
  starting transfers between devices  25.8 us (18%)
  between operations  14.1 us (10%)
  Pallas kernels  11.2 us (8%)
    all_gather x1, waiting for transfers between devices, per_device(): grads = lax.all_gather(token_grads, 'loc', axis=0, tiled=True)  30.6 us
    all_to_all x1, waiting for transfers between devices, per_device(): lax.all_to_all(sums, 'grp', split_axis=0, concat_axis=0, tiled=True)  30.3 us
    all_gather x1, blocking collectives, per_device(): ids = lax.all_gather(row_id, 'loc', axis=0, tiled=True)  29.5 us
    all_to_all x1, starting transfers between devices, per_device(): lax.all_to_all(tag.reshape(groups, 1, 128), 'grp', split_axis=0, concat_a...  13.1 us
    all_to_all x1, starting transfers between devices, per_device(): lax.all_to_all(sums, 'grp', split_axis=0, concat_axis=0, tiled=True)  12.7 us
    pallas_call x1, Pallas kernels, combine(): pl.pallas_call(combine_kernel, grid=(steps,), out_shape=jax.ShapeDtypeStr...  6.69 us
  transfers between devices with their start and end apart: 3, of which 2 were waited for; matrix products, arithmetic and copies ran while one was open for 0% of the time, Pallas kernels for 6%

profile of v1, /device:TPU:34, one launch (start us, length us, event | category | flops | bytes accessed | tf_op | source)
XLA Modules:
  0.0 144.1 jit_solution(14327813566417362723)
XLA Ops:
  7.2 0.0 all-gather.3.cloned.1.call-start
  7.2 0.7 all-gather.3.cloned.1.call-update
  7.9 0.7 add_bitcast_fusion
  8.6 29.5 %all-gather = s32[16,2,128]{2,1,0:T(2,128)S(1)} all-gather(s32[1,2,128]{2,1,0:T(2,128)S(1)} %add_bitcast_fusion), channel_id=1, replica_groups=mesh['grp'=64,'loc'=16] {'loc'}, dimensions={0}, use_global_device_ids=true | all-gather | bytes 17408 | tf_op jit(solution)/shard_map/all_gather | solution.py:198
  38.1 2.0 %shard_map.94 = (bf16[256,2048]{1,0:T(8,128)(2,1)S(1)}, s32[64,128]{1,0:T(8,128)}) custom-call(s32[1]{0:T(128)} %bitcast.me_ref, s32[32,128]{1,0:T(8,128)S(1)} %bitcast.11), custom_call_target="tpu_custom_call" | custom-call | flops 20000000 | bytes 2000000 | tf_op jit(solution)/shard_map/pallas_call | solution.py:124
  40.1 0.0 copy-start
  40.1 1.1 copy-done
  41.2 13.1 %all-to-all-start = ((s32[64,1,128]{2,1,0:T(1,128)}), s32[64,1,128]{2,1,0:T(1,128)S(1)}, u32[]{:S(2)}, u32[]{:S(2)}) async-start(s32[64,1,128]{2,1,0:T(1,128)} %bitcast.5), calls=%async_computation | async-start | bytes 65536 | tf_op jit(solution)/shard_map/all_to_all | solution.py:201
  54.3 30.6 %all-gather.3.cloned.1.call-done.low_ref.high_ref = bf16[2048,2048]{1,0:T(8,128)(2,1)} async-done(((bf16[128,2048]{1,0:T(8,128)(2,1)}), bf16[2048,2048]{1,0:T(8,128)(2,1)}) %all-gather.3.cloned.1.call-update) | async-done | bytes 8388624 | tf_op jit(solution)/shard_map/all_gather | solution.py:196
  84.9 0.0 copy-start.1
  84.9 0.0 copy-start.2
  84.9 0.0 copy-start.3
  84.9 6.7 %shard_map.96 = bf16[64,8,1024]{2,1,0:T(8,128)(2,1)} custom-call(bf16[256,2048]{1,0:T(8,128)(2,1)} %copy-done, bf16[2048,2048]{1,0:T(8,128)(2,1)} %all-gather.3.cloned.1.call-done.low_ref.high_ref, bf16[2048,2048]{1,0:T(8,128)(2,1)} %all-gather.3.cloned.1.call-done.low_ref.high_ref), custom_call_target="tpu_custom_call" | custom-call | tf_op jit(solution)/shard_map/pallas_call | solution.py:154
  91.6 0.0 all-to-all-done
  91.6 12.7 %all-to-all-start.1 = ((bf16[64,8,1024]{2,1,0:T(8,128)(2,1)}), bf16[64,8,1024]{2,1,0:T(8,128)(2,1)S(1)}, u32[]{:S(2)}, u32[]{:S(2)}) async-start(bf16[64,8,1024]{2,1,0:T(8,128)(2,1)} %shard_map.96), calls=%async_computation.1 | async-start | bytes 2097152 | tf_op jit(solution)/shard_map/all_to_all | solution.py:206
  104.3 0.2 shard_map.95.member_ref
  104.5 30.3 %all-to-all-done.1.landed_ref = bf16[64,8,1024]{2,1,0:T(8,128)(2,1)S(1)} async-done(((bf16[64,8,1024]{2,1,0:T(8,128)(2,1)}), bf16[64,8,1024]{2,1,0:T(8,128)(2,1)S(1)}, u32[]{:S(2)}, u32[]{:S(2)}) %all-to-all-start.1) | async-done | bytes 1048608 | tf_op jit(solution)/shard_map/all_to_all | solution.py:206
  134.9 0.0 copy-done.1
  134.9 0.0 copy-done.2
  134.9 0.0 copy-done.3
  134.9 2.3 %shard_map.97 = (f32[32,2048]{1,0:T(8,128)}, f32[32,2048]{1,0:T(8,128)}, f32[32,2048]{1,0:T(8,128)}) custom-call(bf16[2,32,512]{2,1,0:T(8,128)(2,1)S(1)} %shard_map.95.member_ref, bf16[64,8,1024]{2,1,0:T(8,128)(2,1)S(1)} %all-to-all-done.1.landed_ref, f32[32,2048]{1,0:T(8,128)S(1)} %copy-done.1, f32[32,2048]{1,0:T(8,128)S(1)} %copy-done.2, ...), custom_call_target="tpu_custom_call" | custom-call | tf_op jit(solution)/shard_map/pallas_call | solution.py:174
Async XLA Ops:
  7.2 77.7 %all-gather.3.cloned.1.call-start = ((), (), s32[]{:S(2)}) async-start(), calls=%async_computation.2 | async-start | bytes 8912896 | tf_op jit(solution)/shard_map/all_gather | solution.py:196
  40.1 1.1 copy-start
  41.2 50.4 %all-to-all-start = ((s32[64,1,128]{2,1,0:T(1,128)}), s32[64,1,128]{2,1,0:T(1,128)S(1)}, u32[]{:S(2)}, u32[]{:S(2)}) async-start(s32[64,1,128]{2,1,0:T(1,128)} %bitcast.5), calls=%async_computation | async-start | bytes 65536 | tf_op jit(solution)/shard_map/all_to_all | solution.py:201
  84.9 49.9 %copy-start.1 = (f32[32,2048]{1,0:T(8,128)S(1)}, f32[32,2048]{1,0:T(8,128)}, u32[]{:S(2)}) copy-start(f32[32,2048]{1,0:T(8,128)} %table_ref.1) | copy-start | bytes 786436
  84.9 49.9 %copy-start.2 = (f32[32,2048]{1,0:T(8,128)S(1)}, f32[32,2048]{1,0:T(8,128)}, u32[]{:S(2)}) copy-start(f32[32,2048]{1,0:T(8,128)} %first_ref.1) | copy-start | bytes 786436
  84.9 49.9 %copy-start.3 = (f32[32,2048]{1,0:T(8,128)S(1)}, f32[32,2048]{1,0:T(8,128)}, u32[]{:S(2)}) copy-start(f32[32,2048]{1,0:T(8,128)} %second_ref.1) | copy-start | bytes 786436
  91.6 43.2 %all-to-all-start.1 = ((bf16[64,8,1024]{2,1,0:T(8,128)(2,1)}), bf16[64,8,1024]{2,1,0:T(8,128)(2,1)S(1)}, u32[]{:S(2)}, u32[]{:S(2)}) async-start(bf16[64,8,1024]{2,1,0:T(8,128)(2,1)} %shard_map.96), calls=%async_computation.1 | async-start | bytes 2097152 | tf_op jit(solution)/shard_map/all_to_all | solution.py:206
Sparse Core Ops, SparseCore 0:
  10.7 74.1 all-gather.2

commit v2 on v0

v2 whole, which is shorter than its diff:
```python
import functools

import jax
import jax.numpy as jnp
from jax import lax
from jax.experimental import pallas as pl
from jax.experimental.pallas import tpu as pltpu
from jax.sharding import PartitionSpec as P

ADAM_STEP = 100
LANES = 128
SLOTS = 4
TAG_ONE = 16
TAG_TWO = 8

beta_one = 0.9
beta_two = 0.999
learn_rate = 0.01
epsilon = 1e-08

VMEM = pl.BlockSpec(memory_space=pltpu.VMEM)
SMEM = pl.BlockSpec(memory_space=pltpu.SMEM)
NT = (((1,), (1,)), ((), ()))


def iota(shape, dim):
    return lax.broadcasted_iota(jnp.int32, shape, dim)


def ones(mask):
    return jnp.where(mask, 1.0, 0.0).astype(jnp.bfloat16)


def dot(a, b):
    return jnp.dot(a, b, preferred_element_type=jnp.float32)


def dot_nt(a, b):
    return lax.dot_general(a, b, NT, preferred_element_type=jnp.float32)


def pack_kernel(locs, cap, me_ref, loc_ref, group_ref, row_ref, grads_ref, out_ref):
    tokens, width = grads_ref.shape
    shift = me_ref[0] % (LANES // cap) * cap
    before = ones(iota((tokens, tokens), 0) < iota((tokens, tokens), 1))
    base = jnp.zeros((locs, 1), jnp.float32)
    select = jnp.zeros((locs * cap, tokens), jnp.float32)
    tags = jnp.zeros((locs * TAG_ONE, LANES), jnp.float32)
    kind = iota((locs * TAG_ONE, tokens), 0) % TAG_ONE
    for j in range(2):
        dest = loc_ref[j : j + 1]
        member = jnp.where(dest == iota((locs, tokens), 0), 1.0, 0.0)
        ahead = dot(member.astype(jnp.bfloat16), before) + base
        base += jnp.sum(member, axis=1, keepdims=True)
        rank = jnp.sum(ahead * member, axis=0, keepdims=True).astype(jnp.int32)
        select += jnp.where(dest * cap + rank == iota((locs * cap, tokens), 0), 1.0, 0.0)
        group = (group_ref[j : j + 1] + 1).astype(jnp.float32)
        row = row_ref[j : j + 1].astype(jnp.float32)
        value = jnp.where(kind == 0, group, jnp.where(kind == 1, row, 0.0))
        value = jnp.where(dest == iota((locs * TAG_ONE, tokens), 0) // TAG_ONE, value, 0.0)
        tags += dot_nt(value.astype(jnp.bfloat16), ones(rank + shift == iota((LANES, tokens), 0)))
    select = select.astype(jnp.bfloat16)
    blocks = width // LANES
    out_ref[:, blocks * cap :, :] = tags.reshape(locs, TAG_ONE, LANES).astype(jnp.bfloat16)
    for c in range(0, blocks, 2):
        part = dot(select, grads_ref[:, c * LANES : (c + 2) * LANES]).astype(jnp.bfloat16)
        for i in range(2):
            piece = part[:, i * LANES : (i + 1) * LANES].reshape(locs, cap, LANES)
            out_ref[:, (c + i) * cap : (c + i + 1) * cap, :] = piece


def combine_kernel(groups, rows, cap, me_ref, came_ref, out_ref):
    locs = came_ref.shape[0]
    blocks = (came_ref.shape[1] - TAG_ONE) // cap
    lines = locs * cap // LANES
    each = locs // lines
    slots = groups * SLOTS
    tags = came_ref[:, blocks * cap :, :].reshape(locs * TAG_ONE, LANES)
    shape = (2 * lines, locs * TAG_ONE)
    source, kind = iota(shape, 1) // TAG_ONE, iota(shape, 1) % TAG_ONE
    pick = ones((source // each == iota(shape, 0) % lines) & (kind == iota(shape, 0) // lines))
    tags = dot(pick, tags).astype(jnp.int32)
    group, row = tags[:lines] - 1, tags[lines:]
    present = jnp.zeros((groups, rows), jnp.float32)
    for q in range(lines):
        in_group = ones(group[q : q + 1] == iota((groups, LANES), 0))
        in_row = ones(row[q : q + 1] == iota((rows, LANES), 0))
        present += dot_nt(in_group, in_row)
    below = ones(iota((rows, rows), 0) < iota((rows, rows), 1))
    spread = ones(iota((slots, groups), 0) // SLOTS == iota((slots, groups), 1))
    hits = dot(spread, ones(present > 0.5))
    rank = dot(hits.astype(jnp.bfloat16), below).astype(jnp.int32)
    mine = (hits > 0.5) & (rank == iota((slots, rows), 0) % SLOTS)
    slot_row = jnp.max(jnp.where(mine, iota((slots, rows), 1), -1), axis=1, keepdims=True)
    code = jnp.where(slot_row >= 0, iota((slots, 1), 0) // SLOTS * rows + slot_row, -1)
    select = jnp.concatenate(
        [ones(group[q : q + 1] * rows + row[q : q + 1] == code) for q in range(lines)], axis=1
    )
    lane = iota((slots, LANES), 1)
    mark = (lane // 16 == me_ref[0] % 8) & (lane % SLOTS == iota((slots, LANES), 0) % SLOTS)
    mark = jnp.where(mark, (slot_row + 1).astype(jnp.float32), 0.0).astype(jnp.bfloat16)
    shape = (groups * TAG_TWO, slots)
    place = ones((iota(shape, 0) == iota(shape, 1) // SLOTS * TAG_TWO))
    tail = dot(place, mark).reshape(groups, TAG_TWO, LANES)
    out_ref[:, blocks * SLOTS :, :] = tail.astype(jnp.bfloat16)
    top = iota((slots, LANES), 0) % 8 < SLOTS
    for c in range(0, blocks, 4):
        pairs = []
        for b in (c, c + 2):
            part = jnp.concatenate(
                [came_ref[:, i * cap : (i + 1) * cap, :].reshape(locs * cap, LANES) for i in (b, b + 1)], axis=1
            )
            part = dot(select, part)
            low, high = part[:, :LANES], part[:, LANES:]
            even = jnp.where(top, low, pltpu.roll(high, SLOTS, 0)).reshape(slots // 8, 1, 8, LANES)
            odd = jnp.where(top, pltpu.roll(low, slots - SLOTS, 0), high).reshape(slots // 8, 1, 8, LANES)
            pairs.append(jnp.concatenate([even, odd], axis=1).reshape(groups, 8, LANES))
        out_ref[:, c * SLOTS : (c + 4) * SLOTS, :] = jnp.concatenate(pairs, axis=1).astype(jnp.bfloat16)


def update_kernel(landed_ref, table_ref, first_ref, second_ref, t_out, f_out, s_out):
    groups = landed_ref.shape[0]
    rows, width = table_ref.shape
    blocks = width // LANES
    lines = groups // 8
    tags = landed_ref[:, blocks * SLOTS :, :].astype(jnp.float32).reshape(groups * TAG_TWO, LANES)
    shape = (lines, groups * TAG_TWO)
    source, kind = iota(shape, 1) // TAG_TWO, iota(shape, 1) % TAG_TWO
    pick = ones((source // 8 == iota(shape, 0)) & (kind == 0))
    tags = dot(pick, tags.astype(jnp.bfloat16)).astype(jnp.int32) - 1
    shape = (4 * rows, LANES)
    target = iota(shape, 0) % rows
    same_block = iota(shape, 0) // rows == iota(shape, 1) % 16 // SLOTS
    member = jnp.concatenate(
        [ones((tags[i : i + 1] == target) & same_block) for i in range(lines)], axis=1
    )
    touched = jnp.max(member[:rows].astype(jnp.float32), axis=1, keepdims=True) > 0.5
    corr_one = 1.0 - beta_one**ADAM_STEP
    corr_two = 1.0 - beta_two**ADAM_STEP
    for c in range(0, blocks, 8):
        part = jnp.concatenate(
            [
                landed_ref[:, i * SLOTS : (i + 4) * SLOTS, :].reshape(groups * 4 * SLOTS, LANES)
                for i in (c, c + 4)
            ],
            axis=1,
        )
        part = dot(member, part)
        for i in range(8):
            grad = part[i % 4 * rows : (i % 4 + 1) * rows, i // 4 * LANES : (i // 4 + 1) * LANES]
            at = slice((c + i) * LANES, (c + i + 1) * LANES)
            first, second, table = first_ref[:, at], second_ref[:, at], table_ref[:, at]
            first_next = beta_one * first + (1.0 - beta_one) * grad
            second_next = beta_two * second + (1.0 - beta_two) * grad * grad
            update = learn_rate * (first_next / corr_one) / (jnp.sqrt(second_next / corr_two) + epsilon)
            t_out[:, at] = jnp.where(touched, table - update, table)
            f_out[:, at] = jnp.where(touched, first_next, first)
            s_out[:, at] = jnp.where(touched, second_next, second)


PARAMS = pltpu.CompilerParams(vmem_limit_bytes=32 << 20)
WIDE = pltpu.CompilerParams(vmem_limit_bytes=60 << 20)


def pack(me, dest, group, row, grads, locs, cap):
    width = grads.shape[1]
    shape = (locs, width // LANES * cap + TAG_ONE, LANES)
    return pl.pallas_call(
        functools.partial(pack_kernel, locs, cap),
        out_shape=jax.ShapeDtypeStruct(shape, jnp.bfloat16),
        in_specs=[SMEM, VMEM, VMEM, VMEM, VMEM],
        out_specs=VMEM,
        compiler_params=WIDE,
    )(me, dest, group, row, grads)


def combine(me, came, groups, rows, cap):
    blocks = (came.shape[1] - TAG_ONE) // cap
    shape = (groups, blocks * SLOTS + TAG_TWO, LANES)
    return pl.pallas_call(
        functools.partial(combine_kernel, groups, rows, cap),
        out_shape=jax.ShapeDtypeStruct(shape, jnp.bfloat16),
        in_specs=[SMEM, VMEM],
        out_specs=VMEM,
        compiler_params=PARAMS,
    )(me, came)


def update(landed, table, first, second):
    return pl.pallas_call(
        update_kernel,
        out_shape=(jax.ShapeDtypeStruct(table.shape, table.dtype),) * 3,
        in_specs=[VMEM] * 4,
        out_specs=(VMEM,) * 3,
        compiler_params=PARAMS,
    )(landed, table, first, second)


def per_device(
    token_grads, owner_loc, owner_group, owner_row, embed_table, first_moment, second_moment
):
    locs = lax.axis_size("loc")
    groups = lax.axis_size("grp")
    rows = embed_table.shape[0]
    cap = 4 * token_grads.shape[0] // locs
    at_loc = lax.axis_index("loc").astype(jnp.int32).reshape(1)
    at_group = lax.axis_index("grp").astype(jnp.int32).reshape(1)
    packed = pack(at_loc, owner_loc.T, owner_group.T, owner_row.T, token_grads, locs, cap)
    came = lax.all_to_all(packed, "loc", split_axis=0, concat_axis=0, tiled=True)
    sums = combine(at_group, came, groups, rows, cap)
    landed = lax.all_to_all(sums, "grp", split_axis=0, concat_axis=0, tiled=True)
    return tuple(update(landed, embed_table, first_moment, second_moment))


def solution(mesh):
    rows = P(("grp", "loc"), None)
    return jax.shard_map(
        per_device, mesh=mesh, in_specs=(rows,) * 7, out_specs=(rows,) * 3, check_vma=False
    )
```

time: 175 us -> 121 us (0.69)
  waiting for transfers between devices: 107 us -> 50.6 us
  blocking collectives: 0 us -> 46.1 us
  starting transfers between devices: 41 us -> 16.8 us
  matrix products: 11.6 us -> 0 us
  local copies, waits for them, and re-layouts: 8.27 us -> 0.01 us
  Pallas kernels: 0 us -> 6.38 us
  other arithmetic: 5.59 us -> 0 us
    all_to_all x4 -> x1, waiting for transfers between devices: 107 us -> 50.6 us  [per_device(): lax.all_to_all(packed, 'loc', split_axis=0, concat_axis=0, tiled=True)]
    all_to_all x0 -> x1, blocking collectives: none -> 46.1 us  [per_device(): lax.all_to_all(sums, 'grp', split_axis=0, concat_axis=0, tiled=True)]
    all_to_all x4 -> x1, starting transfers between devices: 41 us -> 16.8 us  [per_device(): lax.all_to_all(packed, 'loc', split_axis=0, concat_axis=0, tiled=True)]
    dot_general x3 -> x0, matrix products: 11.6 us -> none  [the longest x1 6.93 us: per_device(): jnp.einsum('grs,gsd->grd', member.astype(jnp.bfloat16), landed, preferred...]
    pallas_call x0 -> x3, Pallas kernels: none -> 6.38 us  [the longest x1 3.34 us: pack(): pl.pallas_call(functools.partial(pack_kernel, locs, cap), out_shape=jax.S...]
    scatter x2 -> x0, local copies, waits for them, and re-layouts: 3.84 us -> none  [the longest x1 2.45 us: per_device(): tag_two = jnp.full((slots_two + 1,), -1, jnp.int32).at[slot_two].set(arri...]
    all_to_all x3 -> x0, local copies, waits for them, and re-layouts: 1.91 us -> none  [the longest x2 1.2 us: per_device(): lax.all_to_all(tag_one.reshape(loc_count, cap_loc), 'loc', split_axis=0,...]
    another operation x4 -> x0, other arithmetic: 1.86 us -> none
  transfers between devices with their start and end apart: 4 -> 1, of which waited for: 4 -> 1; matrix products, arithmetic and copies ran while one was open for 6% -> 0% of each run, Pallas kernels for 0% -> 0%
where the time goes in v2:
time: 121 us
  waiting for transfers between devices  50.6 us (42%)
  blocking collectives  46.1 us (38%)
  starting transfers between devices  16.8 us (14%)
  Pallas kernels  6.38 us (5%)
    all_to_all x1, waiting for transfers between devices, per_device(): lax.all_to_all(packed, 'loc', split_axis=0, concat_axis=0, tiled=True)  50.6 us
    all_to_all x1, blocking collectives, per_device(): lax.all_to_all(sums, 'grp', split_axis=0, concat_axis=0, tiled=True)  46.1 us
    all_to_all x1, starting transfers between devices, per_device(): lax.all_to_all(packed, 'loc', split_axis=0, concat_axis=0, tiled=True)  16.8 us
    pallas_call x1, Pallas kernels, pack(): pl.pallas_call(functools.partial(pack_kernel, locs, cap), out_shape=jax.S...  3.34 us
  transfers between devices with their start and end apart: 1, of which 1 were waited for; matrix products, arithmetic and copies ran while one was open for 0% of the time, Pallas kernels for 0%

profile of v2, /device:TPU:34, one launch (start us, length us, event | category | flops | bytes accessed | tf_op | source)
XLA Modules:
  0.0 120.6 jit_solution(13368482962900040906)
XLA Ops:
  0.6 3.3 %shard_map.94 = bf16[16,528,128]{2,1,0:T(8,128)(2,1)} custom-call(s32[1]{0:T(128)} %bitcast.1.me_ref, s32[2,128]{1,0:T(2,128)} %bitcast.5, s32[2,128]{1,0:T(2,128)} %bitcast.6, s32[2,128]{1,0:T(2,128)} %bitcast.7, bf16[128,2048]{1,0:T(8,128)(2,1)} %grads_ref.1), custom_call_target="tpu_custom_call" | custom-call | tf_op jit(solution)/shard_map/pallas_call | solution.py:168
  4.0 16.8 %all-to-all-start = ((bf16[16,528,128]{2,1,0:T(8,128)(2,1)}), bf16[16,528,128]{2,1,0:T(8,128)(2,1)S(1)}, u32[]{:S(2)}, u32[]{:S(2)}) async-start(bf16[16,528,128]{2,1,0:T(8,128)(2,1)} %shard_map.94), calls=%async_computation | async-start | bytes 4325376 | tf_op jit(solution)/shard_map/all_to_all | solution.py:209
  20.8 50.6 %all-to-all-done.came_ref = bf16[16,528,128]{2,1,0:T(8,128)(2,1)S(1)} async-done(((bf16[16,528,128]{2,1,0:T(8,128)(2,1)}), bf16[16,528,128]{2,1,0:T(8,128)(2,1)S(1)}, u32[]{:S(2)}, u32[]{:S(2)}) %all-to-all-start) | async-done | bytes 2162720 | tf_op jit(solution)/shard_map/all_to_all | solution.py:209
  71.4 0.0 copy-start
  71.4 0.0 copy-start.1
  71.4 0.0 copy-start.2
  71.4 1.6 %shard_map.95 = bf16[64,72,128]{2,1,0:T(8,128)(2,1)S(1)} custom-call(s32[1]{0:T(128)} %bitcast.me_ref, bf16[16,528,128]{2,1,0:T(8,128)(2,1)S(1)} %all-to-all-done.came_ref), custom_call_target="tpu_custom_call" | custom-call | tf_op jit(solution)/shard_map/pallas_call | solution.py:180
  73.0 46.1 %all_to_all.10.landed_ref = bf16[64,72,128]{2,1,0:T(8,128)(2,1)S(1)} all-to-all(bf16[64,72,128]{2,1,0:T(8,128)(2,1)S(1)} %shard_map.95), channel_id=1, replica_groups=mesh['grp'=64,'loc'=16] {'grp'}, dimensions={0} | all-to-all | bytes 2359296 | tf_op jit(solution)/shard_map/all_to_all | solution.py:211
  119.1 0.0 copy-done
  119.1 0.0 copy-done.1
  119.1 0.0 copy-done.2
  119.1 1.5 %shard_map.96 = (f32[32,2048]{1,0:T(8,128)}, f32[32,2048]{1,0:T(8,128)}, f32[32,2048]{1,0:T(8,128)}) custom-call(bf16[64,72,128]{2,1,0:T(8,128)(2,1)S(1)} %all_to_all.10.landed_ref, f32[32,2048]{1,0:T(8,128)S(1)} %copy-done, f32[32,2048]{1,0:T(8,128)S(1)} %copy-done.1, f32[32,2048]{1,0:T(8,128)S(1)} %copy-done.2), custom_call_target="tpu_custom_call" | custom-call | tf_op jit(solution)/shard_map/pallas_call | solution.py:190
Async XLA Ops:
  4.0 67.4 %all-to-all-start = ((bf16[16,528,128]{2,1,0:T(8,128)(2,1)}), bf16[16,528,128]{2,1,0:T(8,128)(2,1)S(1)}, u32[]{:S(2)}, u32[]{:S(2)}) async-start(bf16[16,528,128]{2,1,0:T(8,128)(2,1)} %shard_map.94), calls=%async_computation | async-start | bytes 4325376 | tf_op jit(solution)/shard_map/all_to_all | solution.py:209
  71.4 47.7 %copy-start = (f32[32,2048]{1,0:T(8,128)S(1)}, f32[32,2048]{1,0:T(8,128)}, u32[]{:S(2)}) copy-start(f32[32,2048]{1,0:T(8,128)} %table_ref.1) | copy-start | bytes 786436
  71.4 47.7 %copy-start.1 = (f32[32,2048]{1,0:T(8,128)S(1)}, f32[32,2048]{1,0:T(8,128)}, u32[]{:S(2)}) copy-start(f32[32,2048]{1,0:T(8,128)} %first_ref.1) | copy-start | bytes 786436
  71.4 47.7 %copy-start.2 = (f32[32,2048]{1,0:T(8,128)S(1)}, f32[32,2048]{1,0:T(8,128)}, u32[]{:S(2)}) copy-start(f32[32,2048]{1,0:T(8,128)} %second_ref.1) | copy-start | bytes 786436

commit v3 on v2

v3 whole, which is shorter than its diff:
```python
import functools

import jax
import jax.numpy as jnp
from jax import lax
from jax.experimental import pallas as pl
from jax.experimental.pallas import tpu as pltpu
from jax.sharding import PartitionSpec as P

ADAM_STEP = 100
LANES = 128
SLOTS = 4
TAG_ONE = 16
HALVES = 2
TAG_TWO = 8

beta_one = 0.9
beta_two = 0.999
learn_rate = 0.01
epsilon = 1e-08

VMEM = pl.BlockSpec(memory_space=pltpu.VMEM)
SMEM = pl.BlockSpec(memory_space=pltpu.SMEM)
NT = (((1,), (1,)), ((), ()))


def iota(shape, dim):
    return lax.broadcasted_iota(jnp.int32, shape, dim)


def ones(mask):
    return jnp.where(mask, 1.0, 0.0).astype(jnp.bfloat16)


def dot(a, b):
    return jnp.dot(a, b, preferred_element_type=jnp.float32)


def dot_nt(a, b):
    return lax.dot_general(a, b, NT, preferred_element_type=jnp.float32)


def pack_kernel(chips, me_ref, own_ids_ref, pair_ids_ref, own_ref, pair_ref, *outs):
    tokens, width = own_ref.shape
    full = LANES // 2
    part = full // 2
    far = chips // 2
    chip, core = me_ref[0] // 2, me_ref[0] % 2
    before = ones(iota((tokens, tokens), 0) < iota((tokens, tokens), 1))
    base = jnp.zeros((chips, 1), jnp.float32)
    tags = jnp.zeros((chips * TAG_ONE, LANES), jnp.float32)
    kind = iota((chips * TAG_ONE, tokens), 0) % TAG_ONE
    selects = []
    for ids in (own_ids_ref, pair_ids_ref):
        select = jnp.zeros((chips * full, tokens), jnp.float32)
        for j in range(2):
            dest = ids[j : j + 1]
            step = jnp.where(dest % 2 == core, (dest // 2 - chip + chips) % chips, -1)
            member = jnp.where(step == iota((chips, tokens), 0), 1.0, 0.0)
            ahead = dot(member.astype(jnp.bfloat16), before) + base
            base += jnp.sum(member, axis=1, keepdims=True)
            rank = jnp.sum(ahead * member, axis=0, keepdims=True).astype(jnp.int32)
            select += jnp.where(step * full + rank == iota((chips * full, tokens), 0), 1.0, 0.0)
            group = (ids[2 + j : 3 + j] + 1).astype(jnp.float32)
            row = ids[4 + j : 5 + j].astype(jnp.float32)
            value = jnp.where(kind == 0, group, jnp.where(kind == 1, row, 0.0))
            value = jnp.where(step == iota((chips * TAG_ONE, tokens), 0) // TAG_ONE, value, 0.0)
            spot = rank + step % 2 * full
            tags += dot_nt(value.astype(jnp.bfloat16), ones(spot == iota((LANES, tokens), 0)))
        selects.append(select.astype(jnp.bfloat16))
    select = jnp.concatenate(selects, axis=1)
    tags = tags.astype(jnp.bfloat16)
    blocks = width // LANES // HALVES
    steps = [d for d in range(chips) if d != far]
    for h in range(HALVES):
        into = dict(zip(steps, outs[h * len(steps) : (h + 1) * len(steps)]))
        tail = blocks * full + (TAG_ONE if h == 0 else 0)
        if h == 0:
            for d in steps:
                into[d][blocks * full : tail, :] = tags[d * TAG_ONE : (d + 1) * TAG_ONE]
            for d in (1, chips - 1):
                into[d][tail + blocks * part :, :] = tags[far * TAG_ONE : (far + 1) * TAG_ONE]
        for c in range(0, blocks, 2):
            at = slice((h * blocks + c) * LANES, (h * blocks + c + 2) * LANES)
            grads = jnp.concatenate([own_ref[:, at], pair_ref[:, at]], axis=0)
            packed = dot(select, grads).astype(jnp.bfloat16)
            for i in range(2):
                piece = packed[:, i * LANES : (i + 1) * LANES]
                for d in steps:
                    into[d][(c + i) * full : (c + i + 1) * full, :] = piece[d * full : (d + 1) * full]
                for d, start in ((1, far * full), (chips - 1, far * full + part)):
                    into[d][tail + (c + i) * part : tail + (c + i + 1) * part, :] = piece[start : start + part]


def sum_slots(groups, blocks, select, blocks_of, out_ref):
    slots = groups * SLOTS
    top = iota((slots, LANES), 0) % 8 < SLOTS
    for c in range(0, blocks, 4):
        pairs = []
        for b in (c, c + 2):
            came = dot(select, jnp.concatenate([blocks_of(b), blocks_of(b + 1)], axis=1))
            low, high = came[:, :LANES], came[:, LANES:]
            even = jnp.where(top, low, pltpu.roll(high, SLOTS, 0)).reshape(slots // 8, 1, 8, LANES)
            odd = jnp.where(top, pltpu.roll(low, slots - SLOTS, 0), high).reshape(slots // 8, 1, 8, LANES)
            pairs.append(jnp.concatenate([even, odd], axis=1).reshape(groups, 8, LANES))
        out_ref[:, c * SLOTS : (c + 4) * SLOTS, :] = jnp.concatenate(pairs, axis=1).astype(jnp.bfloat16)


def column_blocks(came):
    full = LANES // 2
    sizes = [full // 2 if i in (len(came) // 2, len(came) // 2 + 1) else full for i in range(len(came))]

    def of(c):
        return jnp.concatenate([r[c * n : (c + 1) * n, :] for r, n in zip(came, sizes)], axis=0)

    return of


def plan_kernel(groups, rows, blocks, me_ref, *refs):
    *came, out_ref, select_ref = refs
    full = LANES // 2
    slots = groups * SLOTS
    chips = len(came) - 1
    far = chips // 2
    tails = []
    for d in range(chips):
        at = blocks * (full // 2 if d == far else full)
        tails.append(came[d if d <= far else d + 1][at : at + TAG_ONE, :])
    tags = jnp.concatenate(tails, axis=0)
    lines = chips // 2
    shape = (2 * lines, chips * TAG_ONE)
    source, kind = iota(shape, 1) // TAG_ONE, iota(shape, 1) % TAG_ONE
    pick = ones((source // 2 == iota(shape, 0) % lines) & (kind == iota(shape, 0) // lines))
    tags = dot(pick, tags).astype(jnp.int32)
    group, row = tags[:lines] - 1, tags[lines:]
    present = jnp.zeros((groups, rows), jnp.float32)
    for q in range(lines):
        in_group = ones(group[q : q + 1] == iota((groups, LANES), 0))
        in_row = ones(row[q : q + 1] == iota((rows, LANES), 0))
        present += dot_nt(in_group, in_row)
    below = ones(iota((rows, rows), 0) < iota((rows, rows), 1))
    spread = ones(iota((slots, groups), 0) // SLOTS == iota((slots, groups), 1))
    hits = dot(spread, ones(present > 0.5))
    rank = dot(hits.astype(jnp.bfloat16), below).astype(jnp.int32)
    mine = (hits > 0.5) & (rank == iota((slots, rows), 0) % SLOTS)
    slot_row = jnp.max(jnp.where(mine, iota((slots, rows), 1), -1), axis=1, keepdims=True)
    code = jnp.where(slot_row >= 0, iota((slots, 1), 0) // SLOTS * rows + slot_row, -1)
    select = jnp.concatenate(
        [ones(group[q : q + 1] * rows + row[q : q + 1] == code) for q in range(lines)], axis=1
    )
    select_ref[...] = select
    lane = iota((slots, LANES), 1)
    mark = (lane // 16 == me_ref[0] % 8) & (lane % SLOTS == iota((slots, LANES), 0) % SLOTS)
    mark = jnp.where(mark, (slot_row + 1).astype(jnp.float32), 0.0).astype(jnp.bfloat16)
    shape = (groups * TAG_TWO, slots)
    place = ones(iota(shape, 0) == iota(shape, 1) // SLOTS * TAG_TWO)
    tail = dot(place, mark).reshape(groups, TAG_TWO, LANES)
    out_ref[:, blocks * SLOTS :, :] = tail.astype(jnp.bfloat16)
    sum_slots(groups, blocks, select, column_blocks(came), out_ref)


def sum_kernel(groups, blocks, select_ref, *refs):
    *came, out_ref = refs
    sum_slots(groups, blocks, select_ref[...], column_blocks(came), out_ref)


def update_kernel(low_ref, high_ref, table_ref, first_ref, second_ref, t_out, f_out, s_out):
    groups = low_ref.shape[0]
    rows, width = table_ref.shape
    blocks = width // LANES
    part_blocks = blocks // HALVES
    lines = groups // 8
    tags = low_ref[:, part_blocks * SLOTS :, :].astype(jnp.float32).reshape(groups * TAG_TWO, LANES)
    shape = (lines, groups * TAG_TWO)
    source, kind = iota(shape, 1) // TAG_TWO, iota(shape, 1) % TAG_TWO
    pick = ones((source // 8 == iota(shape, 0)) & (kind == 0))
    tags = dot(pick, tags.astype(jnp.bfloat16)).astype(jnp.int32) - 1
    shape = (4 * rows, LANES)
    target = iota(shape, 0) % rows
    same_block = iota(shape, 0) // rows == iota(shape, 1) % 16 // SLOTS
    member = jnp.concatenate(
        [ones((tags[i : i + 1] == target) & same_block) for i in range(lines)], axis=1
    )
    touched = jnp.max(member[:rows].astype(jnp.float32), axis=1, keepdims=True) > 0.5
    corr_one = 1.0 - beta_one**ADAM_STEP
    corr_two = 1.0 - beta_two**ADAM_STEP
    for c in range(0, blocks, 8):
        half_ref, off = (low_ref, c) if c < part_blocks else (high_ref, c - part_blocks)
        part = jnp.concatenate(
            [
                half_ref[:, i * SLOTS : (i + 4) * SLOTS, :].reshape(groups * 4 * SLOTS, LANES)
                for i in (off, off + 4)
            ],
            axis=1,
        )
        part = dot(member, part)
        for i in range(8):
            grad = part[i % 4 * rows : (i % 4 + 1) * rows, i // 4 * LANES : (i // 4 + 1) * LANES]
            at = slice((c + i) * LANES, (c + i + 1) * LANES)
            first, second, table = first_ref[:, at], second_ref[:, at], table_ref[:, at]
            first_next = beta_one * first + (1.0 - beta_one) * grad
            second_next = beta_two * second + (1.0 - beta_two) * grad * grad
            update = learn_rate * (first_next / corr_one) / (jnp.sqrt(second_next / corr_two) + epsilon)
            t_out[:, at] = jnp.where(touched, table - update, table)
            f_out[:, at] = jnp.where(touched, first_next, first)
            s_out[:, at] = jnp.where(touched, second_next, second)


PARAMS = pltpu.CompilerParams(vmem_limit_bytes=32 << 20)


def pack(me, own_ids, pair_ids, own, pair, chips):
    full = LANES // 2
    blocks = own.shape[1] // LANES // HALVES
    shapes = []
    for h in range(HALVES):
        tag = TAG_ONE if h == 0 else 0
        for d in range(chips):
            if d != chips // 2:
                length = blocks * full + tag
                if d in (1, chips - 1):
                    length += blocks * full // 2 + tag
                shapes.append(jax.ShapeDtypeStruct((length, LANES), jnp.bfloat16))
    outs = pl.pallas_call(
        functools.partial(pack_kernel, chips),
        out_shape=tuple(shapes),
        in_specs=[SMEM, VMEM, VMEM, VMEM, VMEM],
        out_specs=(VMEM,) * len(shapes),
        compiler_params=PARAMS,
    )(me, own_ids, pair_ids, own, pair)
    return outs[: chips - 1], outs[chips - 1 :]


def travel(packed, chips, length):
    def send(block, up):
        moves = [(c * 2 + i, (c + up) % chips * 2 + i) for c in range(chips) for i in range(2)]
        return lax.ppermute(block, "loc", moves)

    far = chips // 2
    steps = [d for d in range(chips) if d != far]
    block = dict(zip(steps, packed))
    came = {0: block[0]}
    for d in (1, chips - 1, 3, chips - 3, 2, chips - 2):
        came[d] = send(block[d], d)
    parts = [send(came[1][length:], far - 1), send(came[chips - 1][length:], far + 1)]
    return [came[d] for d in range(far)] + parts + [came[d] for d in range(far + 1, chips)]


def first_sums(me, came, groups, rows, blocks):
    slots = groups * SLOTS
    return pl.pallas_call(
        functools.partial(plan_kernel, groups, rows, blocks),
        out_shape=(
            jax.ShapeDtypeStruct((groups, blocks * SLOTS + TAG_TWO, LANES), jnp.bfloat16),
            jax.ShapeDtypeStruct((slots, (len(came) - 1) * LANES // 2), jnp.bfloat16),
        ),
        in_specs=[SMEM] + [VMEM] * len(came),
        out_specs=(VMEM, VMEM),
        compiler_params=PARAMS,
    )(me, *came)


def second_sums(select, came, groups, blocks):
    return pl.pallas_call(
        functools.partial(sum_kernel, groups, blocks),
        out_shape=jax.ShapeDtypeStruct((groups, blocks * SLOTS, LANES), jnp.bfloat16),
        in_specs=[VMEM] * (len(came) + 1),
        out_specs=VMEM,
        compiler_params=PARAMS,
    )(select, *came)


def update(low, high, table, first, second):
    return pl.pallas_call(
        update_kernel,
        out_shape=(jax.ShapeDtypeStruct(table.shape, table.dtype),) * 3,
        in_specs=[VMEM] * 5,
        out_specs=(VMEM,) * 3,
        compiler_params=PARAMS,
    )(low, high, table, first, second)


def per_device(
    token_grads, owner_loc, owner_group, owner_row, embed_table, first_moment, second_moment
):
    locs = lax.axis_size("loc")
    groups = lax.axis_size("grp")
    rows, width = embed_table.shape
    chips = locs // 2
    blocks = width // LANES // HALVES
    at_loc = lax.axis_index("loc").astype(jnp.int32).reshape(1)
    at_group = lax.axis_index("grp").astype(jnp.int32).reshape(1)
    ids = jnp.concatenate([owner_loc.T, owner_group.T, owner_row.T], axis=0)
    swap = [(i, i ^ 1) for i in range(locs)]
    pair_ids = lax.ppermute(ids, "loc", swap)
    pair = lax.ppermute(token_grads, "loc", swap)
    low, high = pack(at_loc, ids, pair_ids, token_grads, pair, chips)
    length = blocks * LANES // 2
    low = travel(low, chips, length + TAG_ONE)
    low, high = lax.optimization_barrier((low, high))
    high = travel(high, chips, length)
    low, select = first_sums(at_group, low, groups, rows, blocks)
    low, high[1], high[-1] = lax.optimization_barrier((low, high[1], high[-1]))
    low = lax.all_to_all(low, "grp", split_axis=0, concat_axis=0, tiled=True)
    low, high[0] = lax.optimization_barrier((low, high[0]))
    high = second_sums(select, high, groups, blocks)
    high = lax.all_to_all(high, "grp", split_axis=0, concat_axis=0, tiled=True)
    return tuple(update(low, high, embed_table, first_moment, second_moment))


def solution(mesh):
    rows = P(("grp", "loc"), None)
    return jax.shard_map(
        per_device, mesh=mesh, in_specs=(rows,) * 7, out_specs=(rows,) * 3, check_vma=False
    )
```

time: 121 us -> 146 us (1.21)
  the two profiles are of different devices: /device:TPU:34 before, /device:TPU:2 now
where the time goes in v3:
time: 146 us; the launch traced here: 145 us
  starting transfers between devices  96.5 us (66%)
  blocking collectives  28.8 us (20%)
  waiting for transfers between devices  11.8 us (8%)
  Pallas kernels  5.05 us (3%)
  local copies, waits for them, and re-layouts  1.77 us (1%)
    ppermute x16, starting transfers between devices, send(): return lax.ppermute(block, 'loc', moves)  78.6 us
    all_to_all x1, blocking collectives, per_device(): high = lax.all_to_all(high, 'grp', split_axis=0, concat_axis=0, tiled=True)  28.8 us
    all_to_all x1, starting transfers between devices, per_device(): low = lax.all_to_all(low, 'grp', split_axis=0, concat_axis=0, tiled=True)  13.6 us
    ppermute x16, waiting for transfers between devices, send(): return lax.ppermute(block, 'loc', moves)  10.9 us
  transfers between devices with their start and end apart: 19, of which 6 were waited for; matrix products, arithmetic and copies ran while one was open for 0% of the time, Pallas kernels for 1%

profile of v3, /device:TPU:2, one launch (start us, length us, event | category | flops | bytes accessed | tf_op | source)
XLA Modules:
  0.0 144.8 jit_solution(13087048838600603807)
XLA Ops:
  0.6 1.9 %collective-permute-start.1 = (bf16[128,2048]{1,0:T(8,128)(2,1)}, bf16[128,2048]{1,0:T(8,128)(2,1)S(1)}, u32[]{:S(2)}, u32[]{:S(2)}) collective-permute-start(bf16[128,2048]{1,0:T(8,128)(2,1)} %own_ref.1), channel_id=1, source_target_pairs={{0,1},{1,0},{2,3},{3,2},{4,5},{5,4},{6,7},{7,6},{8,9},{9,8},{10,11... | collective-permute-start | bytes 1572872 | tf_op jit(solution)/shard_map/ppermute | solution.py:296
  3.3 2.4 %collective-permute-start = (s32[6,128]{1,0:T(8,128)S(1)}, s32[6,128]{1,0:T(8,128)S(1)}, u32[]{:S(2)}, u32[]{:S(2)}) collective-permute-start(s32[6,128]{1,0:T(8,128)S(1)} %pad_add_fusion.own_ids_ref), channel_id=1, source_target_pairs={{0,1},{1,0},{2,3},{3,2},{4,5},{5,4},{6,7},{7,6},{8,9},{9,8},{10,11... | collective-permute-start | bytes 9224 | tf_op jit(solution)/shard_map/ppermute | solution.py:295
  8.5 5.2 %collective-permute-start.2 = (bf16[800,128]{1,0:T(8,128)(2,1)S(1)}, bf16[800,128]{1,0:T(8,128)(2,1)S(1)}, u32[]{:S(2)}, u32[]{:S(2)}) collective-permute-start(bf16[800,128]{1,0:T(8,128)(2,1)S(1)} %get-tuple-element.41), channel_id=1, source_target_pairs={{0,2},{1,3},{2,4},{3,5},{4,6},{5,7},{6,8},{7,9},{8,10},{9,11},{10,... | collective-permute-start | bytes 614408 | tf_op jit(solution)/shard_map/ppermute | solution.py:237
  13.7 14.0 %collective-permute-start.6 = (bf16[800,128]{1,0:T(8,128)(2,1)S(1)}, bf16[800,128]{1,0:T(8,128)(2,1)S(1)}, u32[]{:S(2)}, u32[]{:S(2)}) collective-permute-start(bf16[800,128]{1,0:T(8,128)(2,1)S(1)} %get-tuple-element.44), channel_id=1, source_target_pairs={{0,14},{1,15},{2,0},{3,1},{4,2},{5,3},{6,4},{7,5},{8,6},{9,7},{10,... | collective-permute-start | bytes 614408 | tf_op jit(solution)/shard_map/ppermute | solution.py:237
  27.8 1.9 %collective-permute-start.3 = (bf16[528,128]{1,0:T(8,128)(2,1)S(1)}, bf16[528,128]{1,0:T(8,128)(2,1)S(1)}, u32[]{:S(2)}, u32[]{:S(2)}) collective-permute-start(bf16[528,128]{1,0:T(8,128)(2,1)S(1)} %get-tuple-element.42), channel_id=1, source_target_pairs={{0,4},{1,5},{2,6},{3,7},{4,8},{5,9},{6,10},{7,11},{8,12},{9,13},{1... | collective-permute-start | bytes 405512 | tf_op jit(solution)/shard_map/ppermute | solution.py:237
  29.7 3.9 %collective-permute-start.4 = (bf16[528,128]{1,0:T(8,128)(2,1)S(1)}, bf16[528,128]{1,0:T(8,128)(2,1)S(1)}, u32[]{:S(2)}, u32[]{:S(2)}) collective-permute-start(bf16[528,128]{1,0:T(8,128)(2,1)S(1)} %get-tuple-element.43), channel_id=1, source_target_pairs={{0,6},{1,7},{2,8},{3,9},{4,10},{5,11},{6,12},{7,13},{8,14},{9,15},... | collective-permute-start | bytes 405512 | tf_op jit(solution)/shard_map/ppermute | solution.py:237
  33.6 5.0 %collective-permute-start.8 = (bf16[528,128]{1,0:T(8,128)(2,1)S(1)}, bf16[528,128]{1,0:T(8,128)(2,1)S(1)}, u32[]{:S(2)}, u32[]{:S(2)}) collective-permute-start(bf16[528,128]{1,0:T(8,128)(2,1)S(1)} %get-tuple-element.45), channel_id=1, source_target_pairs={{0,10},{1,11},{2,12},{3,13},{4,14},{5,15},{6,0},{7,1},{8,2},{9,3},... | collective-permute-start | bytes 405512 | tf_op jit(solution)/shard_map/ppermute | solution.py:237
  38.6 6.0 %collective-permute-start.9 = (bf16[528,128]{1,0:T(8,128)(2,1)S(1)}, bf16[528,128]{1,0:T(8,128)(2,1)S(1)}, u32[]{:S(2)}, u32[]{:S(2)}) collective-permute-start(bf16[528,128]{1,0:T(8,128)(2,1)S(1)} %get-tuple-element.46), channel_id=1, source_target_pairs={{0,12},{1,13},{2,14},{3,15},{4,0},{5,1},{6,2},{7,3},{8,4},{9,5},{1... | collective-permute-start | bytes 405512 | tf_op jit(solution)/shard_map/ppermute | solution.py:237
  44.6 1.9 %collective-permute-start.5 = (bf16[272,128]{1,0:T(8,128)(2,1)S(1)}, bf16[272,128]{1,0:T(8,128)(2,1)S(1)}, u32[]{:S(2)}, u32[]{:S(2)}) collective-permute-start(bf16[272,128]{1,0:T(8,128)(2,1)S(1)} %slice.16), channel_id=1, source_target_pairs={{0,6},{1,7},{2,8},{3,9},{4,10},{5,11},{6,12},{7,13},{8,14},{9,15},... | collective-permute-start | bytes 208904 | tf_op jit(solution)/shard_map/ppermute | solution.py:237
  46.6 6.9 %collective-permute-start.7 = (bf16[272,128]{1,0:T(8,128)(2,1)S(1)}, bf16[272,128]{1,0:T(8,128)(2,1)S(1)}, u32[]{:S(2)}, u32[]{:S(2)}) collective-permute-start(bf16[272,128]{1,0:T(8,128)(2,1)S(1)} %slice.17), channel_id=1, source_target_pairs={{0,10},{1,11},{2,12},{3,13},{4,14},{5,15},{6,0},{7,1},{8,2},{9,3},... | collective-permute-start | bytes 208904 | tf_op jit(solution)/shard_map/ppermute | solution.py:237
  53.5 2.7 %collective-permute-done.9.refs_7_ = bf16[528,128]{1,0:T(8,128)(2,1)S(1)} collective-permute-done((bf16[528,128]{1,0:T(8,128)(2,1)S(1)}, bf16[528,128]{1,0:T(8,128)(2,1)S(1)}, u32[]{:S(2)}, u32[]{:S(2)}) %collective-permute-start.9) | collective-permute-done | bytes 135200 | tf_op jit(solution)/shard_map/ppermute | solution.py:237
  57.7 6.1 %collective-permute-start.10 = (bf16[768,128]{1,0:T(8,128)(2,1)S(1)}, bf16[768,128]{1,0:T(8,128)(2,1)S(1)}, u32[]{:S(2)}, u32[]{:S(2)}) collective-permute-start(bf16[768,128]{1,0:T(8,128)(2,1)S(1)} %get-tuple-element.64), channel_id=1, source_target_pairs={{0,2},{1,3},{2,4},{3,5},{4,6},{5,7},{6,8},{7,9},{8,10},{9,11},{10,... | collective-permute-start | bytes 589832 | tf_op jit(solution)/shard_map/ppermute | solution.py:237
  63.8 1.9 %collective-permute-start.11 = (bf16[768,128]{1,0:T(8,128)(2,1)S(1)}, bf16[768,128]{1,0:T(8,128)(2,1)S(1)}, u32[]{:S(2)}, u32[]{:S(2)}) collective-permute-start(bf16[768,128]{1,0:T(8,128)(2,1)S(1)} %get-tuple-element.65), channel_id=1, source_target_pairs={{0,14},{1,15},{2,0},{3,1},{4,2},{5,3},{6,4},{7,5},{8,6},{9,7},{10,... | collective-permute-start | bytes 589832 | tf_op jit(solution)/shard_map/ppermute | solution.py:237
  65.8 2.2 %shard_map.95 = (bf16[64,40,128]{2,1,0:T(8,128)(2,1)}, bf16[256,512]{1,0:T(8,128)(2,1)S(1)}) custom-call(s32[1]{0:T(128)} %bitcast.me_ref, bf16[528,128]{1,0:T(8,128)(2,1)S(1)} %get-tuple-element.54.refs_0_, bf16[800,128]{1,0:T(8,128)(2,1)S(1)} %collective-permute-done.2.refs_1_, bf16[528,128]{1,0:T(8,128)(2,1)S(1)} %collective-permute-done.3.refs_2_, ...), custom_call_target="tpu_custom_call" | custom-call | tf_op jit(solution)/shard_map/pallas_call | solution.py:251
  67.9 3.5 %collective-permute-done.11.refs_8_ = bf16[768,128]{1,0:T(8,128)(2,1)S(1)} collective-permute-done((bf16[768,128]{1,0:T(8,128)(2,1)S(1)}, bf16[768,128]{1,0:T(8,128)(2,1)S(1)}, u32[]{:S(2)}, u32[]{:S(2)}) %collective-permute-start.11) | collective-permute-done | bytes 196640 | tf_op jit(solution)/shard_map/ppermute | solution.py:237
  71.4 13.6 %all-to-all-start = ((bf16[64,40,128]{2,1,0:T(8,128)(2,1)}), bf16[64,40,128]{2,1,0:T(8,128)(2,1)S(1)}, u32[]{:S(2)}, u32[]{:S(2)}) async-start(bf16[64,40,128]{2,1,0:T(8,128)(2,1)} %get-tuple-element.66), calls=%async_computation | async-start | bytes 1310720 | tf_op jit(solution)/shard_map/all_to_all | solution.py:304
  85.0 2.8 %collective-permute-start.12 = (bf16[512,128]{1,0:T(8,128)(2,1)S(1)}, bf16[512,128]{1,0:T(8,128)(2,1)S(1)}, u32[]{:S(2)}, u32[]{:S(2)}) collective-permute-start(bf16[512,128]{1,0:T(8,128)(2,1)S(1)} %get-tuple-element.72), channel_id=1, source_target_pairs={{0,4},{1,5},{2,6},{3,7},{4,8},{5,9},{6,10},{7,11},{8,12},{9,13},{1... | collective-permute-start | bytes 393224 | tf_op jit(solution)/shard_map/ppermute | solution.py:237
  87.8 4.9 %collective-permute-start.13 = (bf16[512,128]{1,0:T(8,128)(2,1)S(1)}, bf16[512,128]{1,0:T(8,128)(2,1)S(1)}, u32[]{:S(2)}, u32[]{:S(2)}) collective-permute-start(bf16[512,128]{1,0:T(8,128)(2,1)S(1)} %get-tuple-element.73), channel_id=1, source_target_pairs={{0,6},{1,7},{2,8},{3,9},{4,10},{5,11},{6,12},{7,13},{8,14},{9,15},... | collective-permute-start | bytes 393224 | tf_op jit(solution)/shard_map/ppermute | solution.py:237
  92.7 4.0 %collective-permute-start.16 = (bf16[512,128]{1,0:T(8,128)(2,1)S(1)}, bf16[512,128]{1,0:T(8,128)(2,1)S(1)}, u32[]{:S(2)}, u32[]{:S(2)}) collective-permute-start(bf16[512,128]{1,0:T(8,128)(2,1)S(1)} %get-tuple-element.74), channel_id=1, source_target_pairs={{0,10},{1,11},{2,12},{3,13},{4,14},{5,15},{6,0},{7,1},{8,2},{9,3},... | collective-permute-start | bytes 393224 | tf_op jit(solution)/shard_map/ppermute | solution.py:237
  96.7 5.1 %collective-permute-start.17 = (bf16[512,128]{1,0:T(8,128)(2,1)S(1)}, bf16[512,128]{1,0:T(8,128)(2,1)S(1)}, u32[]{:S(2)}, u32[]{:S(2)}) collective-permute-start(bf16[512,128]{1,0:T(8,128)(2,1)S(1)} %get-tuple-element.75), channel_id=1, source_target_pairs={{0,12},{1,13},{2,14},{3,15},{4,0},{5,1},{6,2},{7,3},{8,4},{9,5},{1... | collective-permute-start | bytes 393224 | tf_op jit(solution)/shard_map/ppermute | solution.py:237
  101.8 1.9 %collective-permute-start.14 = (bf16[256,128]{1,0:T(8,128)(2,1)S(1)}, bf16[256,128]{1,0:T(8,128)(2,1)S(1)}, u32[]{:S(2)}, u32[]{:S(2)}) collective-permute-start(bf16[256,128]{1,0:T(8,128)(2,1)S(1)} %slice.18), channel_id=1, source_target_pairs={{0,6},{1,7},{2,8},{3,9},{4,10},{5,11},{6,12},{7,13},{8,14},{9,15},... | collective-permute-start | bytes 196616 | tf_op jit(solution)/shard_map/ppermute | solution.py:237
  103.8 6.9 %collective-permute-start.15 = (bf16[256,128]{1,0:T(8,128)(2,1)S(1)}, bf16[256,128]{1,0:T(8,128)(2,1)S(1)}, u32[]{:S(2)}, u32[]{:S(2)}) collective-permute-start(bf16[256,128]{1,0:T(8,128)(2,1)S(1)} %slice.19), channel_id=1, source_target_pairs={{0,10},{1,11},{2,12},{3,13},{4,14},{5,15},{6,0},{7,1},{8,2},{9,3},... | collective-permute-start | bytes 196616 | tf_op jit(solution)/shard_map/ppermute | solution.py:237
  110.8 1.8 %collective-permute-done.17.refs_7_ = bf16[512,128]{1,0:T(8,128)(2,1)S(1)} collective-permute-done((bf16[512,128]{1,0:T(8,128)(2,1)S(1)}, bf16[512,128]{1,0:T(8,128)(2,1)S(1)}, u32[]{:S(2)}, u32[]{:S(2)}) %collective-permute-start.17) | collective-permute-done | bytes 131104 | tf_op jit(solution)/shard_map/ppermute | solution.py:237
  114.5 28.8 %all_to_all.10.high_ref = bf16[64,32,128]{2,1,0:T(8,128)(2,1)S(1)} all-to-all(bf16[64,32,128]{2,1,0:T(8,128)(2,1)S(1)} %shard_map.96), channel_id=1, replica_groups=mesh['grp'=64,'loc'=16] {'grp'}, dimensions={0} | all-to-all | bytes 1048576 | tf_op jit(solution)/shard_map/all_to_all | solution.py:307
  (38 shorter events, 8.5 us)
Async XLA Ops:
  0.6 5.9 %collective-permute-start.1 = (bf16[128,2048]{1,0:T(8,128)(2,1)}, bf16[128,2048]{1,0:T(8,128)(2,1)S(1)}, u32[]{:S(2)}, u32[]{:S(2)}) collective-permute-start(bf16[128,2048]{1,0:T(8,128)(2,1)} %own_ref.1), channel_id=1, source_target_pairs={{0,1},{1,0},{2,3},{3,2},{4,5},{5,4},{6,7},{7,6},{8,9},{9,8},{10,11... | collective-permute-start | bytes 1572872 | tf_op jit(solution)/shard_map/ppermute | solution.py:296
  2.6 0.7 copy-start.4
  3.3 3.2 %collective-permute-start = (s32[6,128]{1,0:T(8,128)S(1)}, s32[6,128]{1,0:T(8,128)S(1)}, u32[]{:S(2)}, u32[]{:S(2)}) collective-permute-start(s32[6,128]{1,0:T(8,128)S(1)} %pad_add_fusion.own_ids_ref), channel_id=1, source_target_pairs={{0,1},{1,0},{2,3},{3,2},{4,5},{5,4},{6,7},{7,6},{8,9},{9,8},{10,11... | collective-permute-start | bytes 9224 | tf_op jit(solution)/shard_map/ppermute | solution.py:295
  6.5 1.0 copy-start
  8.5 30.1 %collective-permute-start.2 = (bf16[800,128]{1,0:T(8,128)(2,1)S(1)}, bf16[800,128]{1,0:T(8,128)(2,1)S(1)}, u32[]{:S(2)}, u32[]{:S(2)}) collective-permute-start(bf16[800,128]{1,0:T(8,128)(2,1)S(1)} %get-tuple-element.41), channel_id=1, source_target_pairs={{0,2},{1,3},{2,4},{3,5},{4,6},{5,7},{6,8},{7,9},{8,10},{9,11},{10,... | collective-permute-start | bytes 614408 | tf_op jit(solution)/shard_map/ppermute | solution.py:237
  13.7 30.9 %collective-permute-start.6 = (bf16[800,128]{1,0:T(8,128)(2,1)S(1)}, bf16[800,128]{1,0:T(8,128)(2,1)S(1)}, u32[]{:S(2)}, u32[]{:S(2)}) collective-permute-start(bf16[800,128]{1,0:T(8,128)(2,1)S(1)} %get-tuple-element.44), channel_id=1, source_target_pairs={{0,14},{1,15},{2,0},{3,1},{4,2},{5,3},{6,4},{7,5},{8,6},{9,7},{10,... | collective-permute-start | bytes 614408 | tf_op jit(solution)/shard_map/ppermute | solution.py:237
  27.8 18.8 %collective-permute-start.3 = (bf16[528,128]{1,0:T(8,128)(2,1)S(1)}, bf16[528,128]{1,0:T(8,128)(2,1)S(1)}, u32[]{:S(2)}, u32[]{:S(2)}) collective-permute-start(bf16[528,128]{1,0:T(8,128)(2,1)S(1)} %get-tuple-element.42), channel_id=1, source_target_pairs={{0,4},{1,5},{2,6},{3,7},{4,8},{5,9},{6,10},{7,11},{8,12},{9,13},{1... | collective-permute-start | bytes 405512 | tf_op jit(solution)/shard_map/ppermute | solution.py:237
  29.7 23.8 %collective-permute-start.4 = (bf16[528,128]{1,0:T(8,128)(2,1)S(1)}, bf16[528,128]{1,0:T(8,128)(2,1)S(1)}, u32[]{:S(2)}, u32[]{:S(2)}) collective-permute-start(bf16[528,128]{1,0:T(8,128)(2,1)S(1)} %get-tuple-element.43), channel_id=1, source_target_pairs={{0,6},{1,7},{2,8},{3,9},{4,10},{5,11},{6,12},{7,13},{8,14},{9,15},... | collective-permute-start | bytes 405512 | tf_op jit(solution)/shard_map/ppermute | solution.py:237
  33.6 19.9 %collective-permute-start.8 = (bf16[528,128]{1,0:T(8,128)(2,1)S(1)}, bf16[528,128]{1,0:T(8,128)(2,1)S(1)}, u32[]{:S(2)}, u32[]{:S(2)}) collective-permute-start(bf16[528,128]{1,0:T(8,128)(2,1)S(1)} %get-tuple-element.45), channel_id=1, source_target_pairs={{0,10},{1,11},{2,12},{3,13},{4,14},{5,15},{6,0},{7,1},{8,2},{9,3},... | collective-permute-start | bytes 405512 | tf_op jit(solution)/shard_map/ppermute | solution.py:237
  38.6 17.7 %collective-permute-start.9 = (bf16[528,128]{1,0:T(8,128)(2,1)S(1)}, bf16[528,128]{1,0:T(8,128)(2,1)S(1)}, u32[]{:S(2)}, u32[]{:S(2)}) collective-permute-start(bf16[528,128]{1,0:T(8,128)(2,1)S(1)} %get-tuple-element.46), channel_id=1, source_target_pairs={{0,12},{1,13},{2,14},{3,15},{4,0},{5,1},{6,2},{7,3},{8,4},{9,5},{1... | collective-permute-start | bytes 405512 | tf_op jit(solution)/shard_map/ppermute | solution.py:237
  44.6 11.6 %collective-permute-start.5 = (bf16[272,128]{1,0:T(8,128)(2,1)S(1)}, bf16[272,128]{1,0:T(8,128)(2,1)S(1)}, u32[]{:S(2)}, u32[]{:S(2)}) collective-permute-start(bf16[272,128]{1,0:T(8,128)(2,1)S(1)} %slice.16), channel_id=1, source_target_pairs={{0,6},{1,7},{2,8},{3,9},{4,10},{5,11},{6,12},{7,13},{8,14},{9,15},... | collective-permute-start | bytes 208904 | tf_op jit(solution)/shard_map/ppermute | solution.py:237
  46.6 11.1 %collective-permute-start.7 = (bf16[272,128]{1,0:T(8,128)(2,1)S(1)}, bf16[272,128]{1,0:T(8,128)(2,1)S(1)}, u32[]{:S(2)}, u32[]{:S(2)}) collective-permute-start(bf16[272,128]{1,0:T(8,128)(2,1)S(1)} %slice.17), channel_id=1, source_target_pairs={{0,10},{1,11},{2,12},{3,13},{4,14},{5,15},{6,0},{7,1},{8,2},{9,3},... | collective-permute-start | bytes 208904 | tf_op jit(solution)/shard_map/ppermute | solution.py:237
  57.7 10.2 %collective-permute-start.10 = (bf16[768,128]{1,0:T(8,128)(2,1)S(1)}, bf16[768,128]{1,0:T(8,128)(2,1)S(1)}, u32[]{:S(2)}, u32[]{:S(2)}) collective-permute-start(bf16[768,128]{1,0:T(8,128)(2,1)S(1)} %get-tuple-element.64), channel_id=1, source_target_pairs={{0,2},{1,3},{2,4},{3,5},{4,6},{5,7},{6,8},{7,9},{8,10},{9,11},{10,... | collective-permute-start | bytes 589832 | tf_op jit(solution)/shard_map/ppermute | solution.py:237
  63.8 7.6 %collective-permute-start.11 = (bf16[768,128]{1,0:T(8,128)(2,1)S(1)}, bf16[768,128]{1,0:T(8,128)(2,1)S(1)}, u32[]{:S(2)}, u32[]{:S(2)}) collective-permute-start(bf16[768,128]{1,0:T(8,128)(2,1)S(1)} %get-tuple-element.65), channel_id=1, source_target_pairs={{0,14},{1,15},{2,0},{3,1},{4,2},{5,3},{6,4},{7,5},{8,6},{9,7},{10,... | collective-permute-start | bytes 589832 | tf_op jit(solution)/shard_map/ppermute | solution.py:237
  71.4 39.3 %all-to-all-start = ((bf16[64,40,128]{2,1,0:T(8,128)(2,1)}), bf16[64,40,128]{2,1,0:T(8,128)(2,1)S(1)}, u32[]{:S(2)}, u32[]{:S(2)}) async-start(bf16[64,40,128]{2,1,0:T(8,128)(2,1)} %get-tuple-element.66), calls=%async_computation | async-start | bytes 1310720 | tf_op jit(solution)/shard_map/all_to_all | solution.py:304
  85.0 18.8 %collective-permute-start.12 = (bf16[512,128]{1,0:T(8,128)(2,1)S(1)}, bf16[512,128]{1,0:T(8,128)(2,1)S(1)}, u32[]{:S(2)}, u32[]{:S(2)}) collective-permute-start(bf16[512,128]{1,0:T(8,128)(2,1)S(1)} %get-tuple-element.72), channel_id=1, source_target_pairs={{0,4},{1,5},{2,6},{3,7},{4,8},{5,9},{6,10},{7,11},{8,12},{9,13},{1... | collective-permute-start | bytes 393224 | tf_op jit(solution)/shard_map/ppermute | solution.py:237
  87.8 22.9 %collective-permute-start.13 = (bf16[512,128]{1,0:T(8,128)(2,1)S(1)}, bf16[512,128]{1,0:T(8,128)(2,1)S(1)}, u32[]{:S(2)}, u32[]{:S(2)}) collective-permute-start(bf16[512,128]{1,0:T(8,128)(2,1)S(1)} %get-tuple-element.73), channel_id=1, source_target_pairs={{0,6},{1,7},{2,8},{3,9},{4,10},{5,11},{6,12},{7,13},{8,14},{9,15},... | collective-permute-start | bytes 393224 | tf_op jit(solution)/shard_map/ppermute | solution.py:237
  92.7 18.1 %collective-permute-start.16 = (bf16[512,128]{1,0:T(8,128)(2,1)S(1)}, bf16[512,128]{1,0:T(8,128)(2,1)S(1)}, u32[]{:S(2)}, u32[]{:S(2)}) collective-permute-start(bf16[512,128]{1,0:T(8,128)(2,1)S(1)} %get-tuple-element.74), channel_id=1, source_target_pairs={{0,10},{1,11},{2,12},{3,13},{4,14},{5,15},{6,0},{7,1},{8,2},{9,3},... | collective-permute-start | bytes 393224 | tf_op jit(solution)/shard_map/ppermute | solution.py:237
  96.7 15.9 %collective-permute-start.17 = (bf16[512,128]{1,0:T(8,128)(2,1)S(1)}, bf16[512,128]{1,0:T(8,128)(2,1)S(1)}, u32[]{:S(2)}, u32[]{:S(2)}) collective-permute-start(bf16[512,128]{1,0:T(8,128)(2,1)S(1)} %get-tuple-element.75), channel_id=1, source_target_pairs={{0,12},{1,13},{2,14},{3,15},{4,0},{5,1},{6,2},{7,3},{8,4},{9,5},{1... | collective-permute-start | bytes 393224 | tf_op jit(solution)/shard_map/ppermute | solution.py:237
  101.8 10.7 %collective-permute-start.14 = (bf16[256,128]{1,0:T(8,128)(2,1)S(1)}, bf16[256,128]{1,0:T(8,128)(2,1)S(1)}, u32[]{:S(2)}, u32[]{:S(2)}) collective-permute-start(bf16[256,128]{1,0:T(8,128)(2,1)S(1)} %slice.18), channel_id=1, source_target_pairs={{0,6},{1,7},{2,8},{3,9},{4,10},{5,11},{6,12},{7,13},{8,14},{9,15},... | collective-permute-start | bytes 196616 | tf_op jit(solution)/shard_map/ppermute | solution.py:237
  103.8 10.3 %collective-permute-start.15 = (bf16[256,128]{1,0:T(8,128)(2,1)S(1)}, bf16[256,128]{1,0:T(8,128)(2,1)S(1)}, u32[]{:S(2)}, u32[]{:S(2)}) collective-permute-start(bf16[256,128]{1,0:T(8,128)(2,1)S(1)} %slice.19), channel_id=1, source_target_pairs={{0,10},{1,11},{2,12},{3,13},{4,14},{5,15},{6,0},{7,1},{8,2},{9,3},... | collective-permute-start | bytes 196616 | tf_op jit(solution)/shard_map/ppermute | solution.py:237
  114.5 28.8 %copy-start.1 = (f32[32,2048]{1,0:T(8,128)S(1)}, f32[32,2048]{1,0:T(8,128)}, u32[]{:S(2)}) copy-start(f32[32,2048]{1,0:T(8,128)} %table_ref.1) | copy-start | bytes 786436
  114.5 28.8 %copy-start.2 = (f32[32,2048]{1,0:T(8,128)S(1)}, f32[32,2048]{1,0:T(8,128)}, u32[]{:S(2)}) copy-start(f32[32,2048]{1,0:T(8,128)} %first_ref.1) | copy-start | bytes 786436
  114.5 28.8 %copy-start.3 = (f32[32,2048]{1,0:T(8,128)S(1)}, f32[32,2048]{1,0:T(8,128)}, u32[]{:S(2)}) copy-start(f32[32,2048]{1,0:T(8,128)} %second_ref.1) | copy-start | bytes 786436
  (2 other events, 1.4 us)

commit v4 on v2

--- a/solution.py
+++ b/solution.py
@@ -10,7 +10,7 @@
 ADAM_STEP = 100
 LANES = 128
 SLOTS = 4
-TAG_ONE = 16
+TAG_ONE = 8
 TAG_TWO = 8
 
 beta_one = 0.9
@@ -20,6 +20,7 @@
 
 VMEM = pl.BlockSpec(memory_space=pltpu.VMEM)
 SMEM = pl.BlockSpec(memory_space=pltpu.SMEM)
+ANY = pl.BlockSpec(memory_space=pl.ANY)
 NT = (((1,), (1,)), ((), ()))
 
 
@@ -39,8 +40,10 @@
     return lax.dot_general(a, b, NT, preferred_element_type=jnp.float32)
 
 
-def pack_kernel(locs, cap, me_ref, loc_ref, group_ref, row_ref, grads_ref, out_ref):
+def pack_kernel(locs, cap, me_ref, loc_ref, group_ref, row_ref, from_ref, to_ref, grads_ref, out_ref, sem):
     tokens, width = grads_ref.shape
+    read = pltpu.make_async_copy(from_ref, grads_ref, sem.at[0])
+    read.start()
     shift = me_ref[0] % (LANES // cap) * cap
     before = ones(iota((tokens, tokens), 0) < iota((tokens, tokens), 1))
     base = jnp.zeros((locs, 1), jnp.float32)
@@ -62,11 +65,22 @@
     select = select.astype(jnp.bfloat16)
     blocks = width // LANES
     out_ref[:, blocks * cap :, :] = tags.reshape(locs, TAG_ONE, LANES).astype(jnp.bfloat16)
-    for c in range(0, blocks, 2):
-        part = dot(select, grads_ref[:, c * LANES : (c + 2) * LANES]).astype(jnp.bfloat16)
-        for i in range(2):
-            piece = part[:, i * LANES : (i + 1) * LANES].reshape(locs, cap, LANES)
-            out_ref[:, (c + i) * cap : (c + i + 1) * cap, :] = piece
+    read.wait()
+    half = locs // 2
+    writes = []
+    for h in range(2):
+        dests = slice(h * half, (h + 1) * half)
+        chosen = select[h * half * cap : (h + 1) * half * cap]
+        for c in range(0, blocks, 2):
+            part = dot(chosen, grads_ref[:, c * LANES : (c + 2) * LANES]).astype(jnp.bfloat16)
+            for i in range(2):
+                piece = part[:, i * LANES : (i + 1) * LANES].reshape(half, cap, LANES)
+                out_ref[dests, (c + i) * cap : (c + i + 1) * cap, :] = piece
+        at = pl.ds(h * half, half)
+        writes.append(pltpu.make_async_copy(out_ref.at[at], to_ref.at[at], sem.at[1 + h]))
+        writes[-1].start()
+    for write in writes:
+        write.wait()
 
 
 def combine_kernel(groups, rows, cap, me_ref, came_ref, out_ref):
@@ -75,11 +89,11 @@
     lines = locs * cap // LANES
     each = locs // lines
     slots = groups * SLOTS
-    tags = came_ref[:, blocks * cap :, :].reshape(locs * TAG_ONE, LANES)
+    tags = came_ref[:, blocks * cap :, :].astype(jnp.float32).reshape(locs * TAG_ONE, LANES)
     shape = (2 * lines, locs * TAG_ONE)
     source, kind = iota(shape, 1) // TAG_ONE, iota(shape, 1) % TAG_ONE
     pick = ones((source // each == iota(shape, 0) % lines) & (kind == iota(shape, 0) // lines))
-    tags = dot(pick, tags).astype(jnp.int32)
+    tags = dot(pick, tags.astype(jnp.bfloat16)).astype(jnp.int32)
     group, row = tags[:lines] - 1, tags[lines:]
     present = jnp.zeros((groups, rows), jnp.float32)
     for q in range(lines):
@@ -168,8 +182,13 @@
     return pl.pallas_call(
         functools.partial(pack_kernel, locs, cap),
         out_shape=jax.ShapeDtypeStruct(shape, jnp.bfloat16),
-        in_specs=[SMEM, VMEM, VMEM, VMEM, VMEM],
-        out_specs=VMEM,
+        in_specs=[SMEM, VMEM, VMEM, VMEM, ANY],
+        out_specs=ANY,
+        scratch_shapes=[
+            pltpu.VMEM(grads.shape, jnp.bfloat16),
+            pltpu.VMEM(shape, jnp.bfloat16),
+            pltpu.SemaphoreType.DMA((3,)),
+        ],
         compiler_params=WIDE,
     )(me, dest, group, row, grads)
 

time: 121 us -> 120 us (level)
  no operation moved by 1% of the time
where the time goes in v4:
time: 120 us
  waiting for transfers between devices  49.9 us (42%)
  blocking collectives  46.2 us (38%)
  starting transfers between devices  16.8 us (14%)
  Pallas kernels  6.61 us (6%)
    all_to_all x1, waiting for transfers between devices, per_device(): lax.all_to_all(packed, 'loc', split_axis=0, concat_axis=0, tiled=True)  49.9 us
    all_to_all x1, blocking collectives, per_device(): lax.all_to_all(sums, 'grp', split_axis=0, concat_axis=0, tiled=True)  46.2 us
    all_to_all x1, starting transfers between devices, per_device(): lax.all_to_all(packed, 'loc', split_axis=0, concat_axis=0, tiled=True)  16.8 us
    pallas_call x1, Pallas kernels, pack(): pl.pallas_call(functools.partial(pack_kernel, locs, cap), out_shape=jax.S...  3.57 us
  transfers between devices with their start and end apart: 1, of which 1 were waited for; matrix products, arithmetic and copies ran while one was open for 0% of the time, Pallas kernels for 0%

profile of v4, /device:TPU:34, one launch (start us, length us, event | category | flops | bytes accessed | tf_op | source)
XLA Modules:
  0.0 120.2 jit_solution(16094088841368223294)
XLA Ops:
  0.6 3.6 %shard_map.94 = bf16[16,520,128]{2,1,0:T(8,128)(2,1)} custom-call(s32[1]{0:T(128)} %bitcast.1.me_ref, s32[2,128]{1,0:T(2,128)} %bitcast.5, s32[2,128]{1,0:T(2,128)} %bitcast.6, s32[2,128]{1,0:T(2,128)} %bitcast.7, bf16[128,2048]{1,0:T(8,128)(2,1)} %from_ref.1), custom_call_target="tpu_custom_call" | custom-call | tf_op jit(solution)/shard_map/pallas_call | solution.py:182
  4.2 16.8 %all-to-all-start = ((bf16[16,520,128]{2,1,0:T(8,128)(2,1)}), bf16[16,520,128]{2,1,0:T(8,128)(2,1)S(1)}, u32[]{:S(2)}, u32[]{:S(2)}) async-start(bf16[16,520,128]{2,1,0:T(8,128)(2,1)} %shard_map.94), calls=%async_computation | async-start | bytes 4259840 | tf_op jit(solution)/shard_map/all_to_all | solution.py:228
  21.0 49.9 %all-to-all-done.came_ref = bf16[16,520,128]{2,1,0:T(8,128)(2,1)S(1)} async-done(((bf16[16,520,128]{2,1,0:T(8,128)(2,1)}), bf16[16,520,128]{2,1,0:T(8,128)(2,1)S(1)}, u32[]{:S(2)}, u32[]{:S(2)}) %all-to-all-start) | async-done | bytes 2129952 | tf_op jit(solution)/shard_map/all_to_all | solution.py:228
  70.9 0.0 copy-start
  70.9 0.0 copy-start.1
  70.9 0.0 copy-start.2
  70.9 1.6 %shard_map.95 = bf16[64,72,128]{2,1,0:T(8,128)(2,1)S(1)} custom-call(s32[1]{0:T(128)} %bitcast.me_ref, bf16[16,520,128]{2,1,0:T(8,128)(2,1)S(1)} %all-to-all-done.came_ref), custom_call_target="tpu_custom_call" | custom-call | tf_op jit(solution)/shard_map/pallas_call | solution.py:199
  72.5 46.2 %all_to_all.10.landed_ref = bf16[64,72,128]{2,1,0:T(8,128)(2,1)S(1)} all-to-all(bf16[64,72,128]{2,1,0:T(8,128)(2,1)S(1)} %shard_map.95), channel_id=1, replica_groups=mesh['grp'=64,'loc'=16] {'grp'}, dimensions={0} | all-to-all | bytes 2359296 | tf_op jit(solution)/shard_map/all_to_all | solution.py:230
  118.7 0.0 copy-done
  118.7 0.0 copy-done.1
  118.7 0.0 copy-done.2
  118.7 1.5 %shard_map.96 = (f32[32,2048]{1,0:T(8,128)}, f32[32,2048]{1,0:T(8,128)}, f32[32,2048]{1,0:T(8,128)}) custom-call(bf16[64,72,128]{2,1,0:T(8,128)(2,1)S(1)} %all_to_all.10.landed_ref, f32[32,2048]{1,0:T(8,128)S(1)} %copy-done, f32[32,2048]{1,0:T(8,128)S(1)} %copy-done.1, f32[32,2048]{1,0:T(8,128)S(1)} %copy-done.2), custom_call_target="tpu_custom_call" | custom-call | tf_op jit(solution)/shard_map/pallas_call | solution.py:209
Async XLA Ops:
  4.2 66.7 %all-to-all-start = ((bf16[16,520,128]{2,1,0:T(8,128)(2,1)}), bf16[16,520,128]{2,1,0:T(8,128)(2,1)S(1)}, u32[]{:S(2)}, u32[]{:S(2)}) async-start(bf16[16,520,128]{2,1,0:T(8,128)(2,1)} %shard_map.94), calls=%async_computation | async-start | bytes 4259840 | tf_op jit(solution)/shard_map/all_to_all | solution.py:228
  70.9 47.8 %copy-start = (f32[32,2048]{1,0:T(8,128)S(1)}, f32[32,2048]{1,0:T(8,128)}, u32[]{:S(2)}) copy-start(f32[32,2048]{1,0:T(8,128)} %table_ref.1) | copy-start | bytes 786436
  70.9 47.8 %copy-start.1 = (f32[32,2048]{1,0:T(8,128)S(1)}, f32[32,2048]{1,0:T(8,128)}, u32[]{:S(2)}) copy-start(f32[32,2048]{1,0:T(8,128)} %first_ref.1) | copy-start | bytes 786436
  70.9 47.8 %copy-start.2 = (f32[32,2048]{1,0:T(8,128)S(1)}, f32[32,2048]{1,0:T(8,128)}, u32[]{:S(2)}) copy-start(f32[32,2048]{1,0:T(8,128)} %second_ref.1) | copy-start | bytes 786436

commit v5 on v2

--- a/solution.py
+++ b/solution.py
@@ -10,7 +10,7 @@
 ADAM_STEP = 100
 LANES = 128
 SLOTS = 4
-TAG_ONE = 16
+TAG_ONE = 8
 TAG_TWO = 8
 
 beta_one = 0.9
@@ -20,6 +20,7 @@
 
 VMEM = pl.BlockSpec(memory_space=pltpu.VMEM)
 SMEM = pl.BlockSpec(memory_space=pltpu.SMEM)
+FAR = pl.BlockSpec(memory_space=pltpu.HBM)
 NT = (((1,), (1,)), ((), ()))
 
 
@@ -39,8 +40,18 @@
     return lax.dot_general(a, b, NT, preferred_element_type=jnp.float32)
 
 
-def pack_kernel(locs, cap, me_ref, loc_ref, group_ref, row_ref, grads_ref, out_ref):
+def pack_kernel(locs, cap, me_ref, also_ref, loc_from, group_from, row_from, grads_from, out_ref, *scratch):
+    *arrays, sem = scratch
+    reads = [
+        pltpu.make_async_copy(a, b, sem.at[i])
+        for i, (a, b) in enumerate(zip((loc_from, group_from, row_from, grads_from), arrays))
+    ]
+    for read in reads:
+        read.start()
+    loc_ref, group_ref, row_ref, grads_ref = arrays
     tokens, width = grads_ref.shape
+    for read in reads[:3]:
+        read.wait()
     shift = me_ref[0] % (LANES // cap) * cap
     before = ones(iota((tokens, tokens), 0) < iota((tokens, tokens), 1))
     base = jnp.zeros((locs, 1), jnp.float32)
@@ -61,6 +72,7 @@
         tags += dot_nt(value.astype(jnp.bfloat16), ones(rank + shift == iota((LANES, tokens), 0)))
     select = select.astype(jnp.bfloat16)
     blocks = width // LANES
+    reads[3].wait()
     out_ref[:, blocks * cap :, :] = tags.reshape(locs, TAG_ONE, LANES).astype(jnp.bfloat16)
     for c in range(0, blocks, 2):
         part = dot(select, grads_ref[:, c * LANES : (c + 2) * LANES]).astype(jnp.bfloat16)
@@ -75,11 +87,11 @@
     lines = locs * cap // LANES
     each = locs // lines
     slots = groups * SLOTS
-    tags = came_ref[:, blocks * cap :, :].reshape(locs * TAG_ONE, LANES)
+    tags = came_ref[:, blocks * cap :, :].astype(jnp.float32).reshape(locs * TAG_ONE, LANES)
     shape = (2 * lines, locs * TAG_ONE)
     source, kind = iota(shape, 1) // TAG_ONE, iota(shape, 1) % TAG_ONE
     pick = ones((source // each == iota(shape, 0) % lines) & (kind == iota(shape, 0) // lines))
-    tags = dot(pick, tags).astype(jnp.int32)
+    tags = dot(pick, tags.astype(jnp.bfloat16)).astype(jnp.int32)
     group, row = tags[:lines] - 1, tags[lines:]
     present = jnp.zeros((groups, rows), jnp.float32)
     for q in range(lines):
@@ -159,19 +171,26 @@
 
 
 PARAMS = pltpu.CompilerParams(vmem_limit_bytes=32 << 20)
-WIDE = pltpu.CompilerParams(vmem_limit_bytes=60 << 20)
-
-
-def pack(me, dest, group, row, grads, locs, cap):
+WIDE = pltpu.CompilerParams(vmem_limit_bytes=32 << 20)
+
+
+def pack(me, also, dest, group, row, grads, locs, cap):
     width = grads.shape[1]
     shape = (locs, width // LANES * cap + TAG_ONE, LANES)
     return pl.pallas_call(
         functools.partial(pack_kernel, locs, cap),
         out_shape=jax.ShapeDtypeStruct(shape, jnp.bfloat16),
-        in_specs=[SMEM, VMEM, VMEM, VMEM, VMEM],
+        in_specs=[SMEM, SMEM, FAR, FAR, FAR, FAR],
         out_specs=VMEM,
+        scratch_shapes=[
+            pltpu.VMEM(dest.shape, jnp.int32),
+            pltpu.VMEM(dest.shape, jnp.int32),
+            pltpu.VMEM(dest.shape, jnp.int32),
+            pltpu.VMEM(grads.shape, jnp.bfloat16),
+            pltpu.SemaphoreType.DMA((4,)),
+        ],
         compiler_params=WIDE,
-    )(me, dest, group, row, grads)
+    )(me, also, *(pltpu.with_memory_space_constraint(a, pltpu.HBM) for a in (dest, group, row, grads)))
 
 
 def combine(me, came, groups, rows, cap):
@@ -205,7 +224,7 @@
     cap = 4 * token_grads.shape[0] // locs
     at_loc = lax.axis_index("loc").astype(jnp.int32).reshape(1)
     at_group = lax.axis_index("grp").astype(jnp.int32).reshape(1)
-    packed = pack(at_loc, owner_loc.T, owner_group.T, owner_row.T, token_grads, locs, cap)
+    packed = pack(at_loc, at_group, owner_loc.T, owner_group.T, owner_row.T, token_grads, locs, cap)
     came = lax.all_to_all(packed, "loc", split_axis=0, concat_axis=0, tiled=True)
     sums = combine(at_group, came, groups, rows, cap)
     landed = lax.all_to_all(sums, "grp", split_axis=0, concat_axis=0, tiled=True)

time: 121 us -> 121 us (level)
  blocking collectives: 46.1 us -> 115 us
  waiting for transfers between devices: 50.6 us -> 0 us
  starting transfers between devices: 16.8 us -> 0 us
  Pallas kernels: 6.38 us -> 4.91 us
    all_to_all x0 -> x1, blocking collectives: none -> 69 us  [per_device(): lax.all_to_all(packed, 'loc', split_axis=0, concat_axis=0, tiled=True)]
    all_to_all x1 -> x0, waiting for transfers between devices: 50.6 us -> none  [per_device(): lax.all_to_all(packed, 'loc', split_axis=0, concat_axis=0, tiled=True)]
    all_to_all x1 -> x0, starting transfers between devices: 16.8 us -> none  [per_device(): lax.all_to_all(packed, 'loc', split_axis=0, concat_axis=0, tiled=True)]
    pallas_call x1, Pallas kernels: 3.34 us -> 1.86 us  [pack(): pl.pallas_call(functools.partial(pack_kernel, locs, cap), out_shape=jax.S...]
  transfers between devices with their start and end apart: 1 -> 0, of which waited for: 1 -> 0; matrix products, arithmetic and copies ran while one was open for 0% -> 0% of each run, Pallas kernels for 0% -> 0%
where the time goes in v5:
time: 121 us
  blocking collectives  115 us (95%)
  Pallas kernels  4.91 us (4%)
    all_to_all x1, blocking collectives, per_device(): lax.all_to_all(packed, 'loc', split_axis=0, concat_axis=0, tiled=True)  69 us
    all_to_all x1, blocking collectives, per_device(): lax.all_to_all(sums, 'grp', split_axis=0, concat_axis=0, tiled=True)  46.1 us

profile of v5, /device:TPU:34, one launch (start us, length us, event | category | flops | bytes accessed | tf_op | source)
XLA Modules:
  0.0 120.7 jit_solution(18126249360102612089)
XLA Ops:
  0.6 1.9 %shard_map.94 = bf16[16,520,128]{2,1,0:T(8,128)(2,1)S(1)} custom-call(s32[1]{0:T(128)} %bitcast.1.me_ref, s32[1]{0:T(128)} %bitcast.also_ref.me_ref, s32[2,128]{1,0:T(2,128)} %bitcast.5, s32[2,128]{1,0:T(2,128)} %bitcast.6, s32[2,128]{1,0:T(2,128)} %bitcast.7, bf16[128,2048]{1,0:T(8,128)(2,1)} %grads_from.1), custom_call_target="tpu_custom_call" | custom-call | tf_op jit(solution)/shard_map/pallas_call | solution.py:180
  2.5 69.0 %all_to_all.10.came_ref = bf16[16,520,128]{2,1,0:T(8,128)(2,1)S(1)} all-to-all(bf16[16,520,128]{2,1,0:T(8,128)(2,1)S(1)} %shard_map.94), channel_id=1, replica_groups=mesh['grp'=64,'loc'=16] {'loc'}, dimensions={0} | all-to-all | bytes 4259840 | tf_op jit(solution)/shard_map/all_to_all | solution.py:228
  71.5 0.0 copy-start
  71.5 0.0 copy-start.1
  71.5 0.0 copy-start.2
  71.5 1.6 %shard_map.95 = bf16[64,72,128]{2,1,0:T(8,128)(2,1)S(1)} custom-call(s32[1]{0:T(128)} %bitcast.also_ref.me_ref, bf16[16,520,128]{2,1,0:T(8,128)(2,1)S(1)} %all_to_all.10.came_ref), custom_call_target="tpu_custom_call" | custom-call | tf_op jit(solution)/shard_map/pallas_call | solution.py:199
  73.1 46.1 %all_to_all.11.landed_ref = bf16[64,72,128]{2,1,0:T(8,128)(2,1)S(1)} all-to-all(bf16[64,72,128]{2,1,0:T(8,128)(2,1)S(1)} %shard_map.95), channel_id=1, replica_groups=mesh['grp'=64,'loc'=16] {'grp'}, dimensions={0} | all-to-all | bytes 2359296 | tf_op jit(solution)/shard_map/all_to_all | solution.py:230
  119.2 0.0 copy-done
  119.2 0.0 copy-done.1
  119.2 0.0 copy-done.2
  119.2 1.5 %shard_map.96 = (f32[32,2048]{1,0:T(8,128)}, f32[32,2048]{1,0:T(8,128)}, f32[32,2048]{1,0:T(8,128)}) custom-call(bf16[64,72,128]{2,1,0:T(8,128)(2,1)S(1)} %all_to_all.11.landed_ref, f32[32,2048]{1,0:T(8,128)S(1)} %copy-done, f32[32,2048]{1,0:T(8,128)S(1)} %copy-done.1, f32[32,2048]{1,0:T(8,128)S(1)} %copy-done.2), custom_call_target="tpu_custom_call" | custom-call | tf_op jit(solution)/shard_map/pallas_call | solution.py:209
Async XLA Ops:
  71.5 47.7 %copy-start = (f32[32,2048]{1,0:T(8,128)S(1)}, f32[32,2048]{1,0:T(8,128)}, u32[]{:S(2)}) copy-start(f32[32,2048]{1,0:T(8,128)} %table_ref.1) | copy-start | bytes 786436
  71.5 47.7 %copy-start.1 = (f32[32,2048]{1,0:T(8,128)S(1)}, f32[32,2048]{1,0:T(8,128)}, u32[]{:S(2)}) copy-start(f32[32,2048]{1,0:T(8,128)} %first_ref.1) | copy-start | bytes 786436
  71.5 47.7 %copy-start.2 = (f32[32,2048]{1,0:T(8,128)S(1)}, f32[32,2048]{1,0:T(8,128)}, u32[]{:S(2)}) copy-start(f32[32,2048]{1,0:T(8,128)} %second_ref.1) | copy-start | bytes 786436

commit v6 on v4

--- a/solution.py
+++ b/solution.py
@@ -11,7 +11,8 @@
 LANES = 128
 SLOTS = 4
 TAG_ONE = 8
-TAG_TWO = 8
+PARTS = 4
+TILE = 8
 
 beta_one = 0.9
 beta_two = 0.999
@@ -66,9 +67,9 @@
     blocks = width // LANES
     out_ref[:, blocks * cap :, :] = tags.reshape(locs, TAG_ONE, LANES).astype(jnp.bfloat16)
     read.wait()
-    half = locs // 2
+    half = locs // PARTS
     writes = []
-    for h in range(2):
+    for h in range(PARTS):
         dests = slice(h * half, (h + 1) * half)
         chosen = select[h * half * cap : (h + 1) * half * cap]
         for c in range(0, blocks, 2):
@@ -111,65 +112,80 @@
         [ones(group[q : q + 1] * rows + row[q : q + 1] == code) for q in range(lines)], axis=1
     )
     lane = iota((slots, LANES), 1)
-    mark = (lane // 16 == me_ref[0] % 8) & (lane % SLOTS == iota((slots, LANES), 0) % SLOTS)
-    mark = jnp.where(mark, (slot_row + 1).astype(jnp.float32), 0.0).astype(jnp.bfloat16)
-    shape = (groups * TAG_TWO, slots)
-    place = ones((iota(shape, 0) == iota(shape, 1) // SLOTS * TAG_TWO))
-    tail = dot(place, mark).reshape(groups, TAG_TWO, LANES)
-    out_ref[:, blocks * SLOTS :, :] = tail.astype(jnp.bfloat16)
-    top = iota((slots, LANES), 0) % 8 < SLOTS
-    for c in range(0, blocks, 4):
-        pairs = []
-        for b in (c, c + 2):
-            part = jnp.concatenate(
-                [came_ref[:, i * cap : (i + 1) * cap, :].reshape(locs * cap, LANES) for i in (b, b + 1)], axis=1
-            )
-            part = dot(select, part)
-            low, high = part[:, :LANES], part[:, LANES:]
-            even = jnp.where(top, low, pltpu.roll(high, SLOTS, 0)).reshape(slots // 8, 1, 8, LANES)
-            odd = jnp.where(top, pltpu.roll(low, slots - SLOTS, 0), high).reshape(slots // 8, 1, 8, LANES)
-            pairs.append(jnp.concatenate([even, odd], axis=1).reshape(groups, 8, LANES))
-        out_ref[:, c * SLOTS : (c + 4) * SLOTS, :] = jnp.concatenate(pairs, axis=1).astype(jnp.bfloat16)
+    mark = (lane // 16 == me_ref[0] // 2 % 8) & (lane % SLOTS == iota((slots, LANES), 0) % SLOTS)
+    mark = jnp.where(mark, (slot_row + 1).astype(jnp.float32), 0.0)
+    top = iota((slots, LANES), 0) % TILE < SLOTS
+    pairs = groups // 2
+    sums = {blocks: mark}
+    tiles = {}
+
+    def tile(low, high):
+        return jnp.where(top, low, high).reshape(pairs, TILE, LANES)
+
+    def up(x):
+        return pltpu.roll(x, slots - SLOTS, 0)
+
+    def store(t):
+        both = jnp.concatenate([tiles.pop(t), tiles.pop(t + 1)], axis=1)
+        out_ref[:, t * TILE : (t + 2) * TILE, :] = both.astype(jnp.bfloat16)
+
+    for c in range(0, blocks, 2):
+        part = jnp.concatenate(
+            [came_ref[:, i * cap : (i + 1) * cap, :].reshape(locs * cap, LANES) for i in (c, c + 1)], axis=1
+        )
+        part = dot(select, part)
+        sums[c], sums[c + 1] = part[:, :LANES], part[:, LANES:]
+        tiles[c // 2] = tile(sums[c], pltpu.roll(sums[c + 1], SLOTS, 0))
+        tiles[blocks // 2 + c // 2] = tile(up(sums[c - 1]), sums[c]) if c else tile(mark, sums[0])
+        if c % 4 == 2:
+            store(c // 2 - 1)
+            store(blocks // 2 + c // 2 - 1)
+    out_ref[:, blocks * TILE :, :] = tile(up(sums[blocks - 1]), mark).astype(jnp.bfloat16)
 
 
 def update_kernel(landed_ref, table_ref, first_ref, second_ref, t_out, f_out, s_out):
-    groups = landed_ref.shape[0]
+    pairs = landed_ref.shape[0]
     rows, width = table_ref.shape
     blocks = width // LANES
-    lines = groups // 8
-    tags = landed_ref[:, blocks * SLOTS :, :].astype(jnp.float32).reshape(groups * TAG_TWO, LANES)
-    shape = (lines, groups * TAG_TWO)
-    source, kind = iota(shape, 1) // TAG_TWO, iota(shape, 1) % TAG_TWO
-    pick = ones((source // 8 == iota(shape, 0)) & (kind == 0))
-    tags = dot(pick, tags.astype(jnp.bfloat16)).astype(jnp.int32) - 1
-    shape = (4 * rows, LANES)
-    target = iota(shape, 0) % rows
-    same_block = iota(shape, 0) // rows == iota(shape, 1) % 16 // SLOTS
-    member = jnp.concatenate(
-        [ones((tags[i : i + 1] == target) & same_block) for i in range(lines)], axis=1
-    )
-    touched = jnp.max(member[:rows].astype(jnp.float32), axis=1, keepdims=True) > 0.5
+    lines = pairs // 8
+    shape = (lines, pairs * TILE)
+    source, line = iota(shape, 1) // TILE // 8, iota(shape, 0)
+    target = iota((4 * rows, LANES), 0) % rows
+    same_block = iota((4 * rows, LANES), 0) // rows == iota((4 * rows, LANES), 1) % 16 // SLOTS
+    members = []
+    for at, last in ((blocks // 2 * TILE, False), (blocks * TILE, True)):
+        tags = landed_ref[:, at : at + TILE, :].astype(jnp.float32).reshape(pairs * TILE, LANES)
+        low = iota(shape, 1) % TILE < SLOTS
+        pick = ones((source == line) & (jnp.logical_not(low) if last else low))
+        tags = dot(pick, tags.astype(jnp.bfloat16)).astype(jnp.int32) - 1
+        members.append(
+            jnp.concatenate([ones((tags[i : i + 1] == target) & same_block) for i in range(lines)], axis=1)
+        )
+    found = members[0][:rows].astype(jnp.float32) + members[1][:rows].astype(jnp.float32)
+    touched = jnp.max(found, axis=1, keepdims=True) > 0.5
+    halves = []
+    for t in range(0, blocks, 4):
+        part = [
+            landed_ref[:, i * TILE : (i + 2) * TILE, :].reshape(pairs * 2 * TILE, LANES) for i in (t, t + 2)
+        ]
+        part = dot(members[t >= blocks // 2], jnp.concatenate(part, axis=1))
+        for i in range(8):
+            halves.append(part[i % 4 * rows : (i % 4 + 1) * rows, i // 4 * LANES : (i // 4 + 1) * LANES])
+    end = landed_ref[:, blocks * TILE :, :].astype(jnp.float32)
+    end = jnp.concatenate([end, jnp.zeros_like(end)], axis=1).reshape(pairs * 2 * TILE, LANES)
+    halves.append(dot(members[1][:rows], end.astype(jnp.bfloat16)))
     corr_one = 1.0 - beta_one**ADAM_STEP
     corr_two = 1.0 - beta_two**ADAM_STEP
-    for c in range(0, blocks, 8):
-        part = jnp.concatenate(
-            [
-                landed_ref[:, i * SLOTS : (i + 4) * SLOTS, :].reshape(groups * 4 * SLOTS, LANES)
-                for i in (c, c + 4)
-            ],
-            axis=1,
-        )
-        part = dot(member, part)
-        for i in range(8):
-            grad = part[i % 4 * rows : (i % 4 + 1) * rows, i // 4 * LANES : (i // 4 + 1) * LANES]
-            at = slice((c + i) * LANES, (c + i + 1) * LANES)
-            first, second, table = first_ref[:, at], second_ref[:, at], table_ref[:, at]
-            first_next = beta_one * first + (1.0 - beta_one) * grad
-            second_next = beta_two * second + (1.0 - beta_two) * grad * grad
-            update = learn_rate * (first_next / corr_one) / (jnp.sqrt(second_next / corr_two) + epsilon)
-            t_out[:, at] = jnp.where(touched, table - update, table)
-            f_out[:, at] = jnp.where(touched, first_next, first)
-            s_out[:, at] = jnp.where(touched, second_next, second)
+    for c in range(blocks):
+        grad = halves[c] + halves[blocks + 1 + c]
+        at = slice(c * LANES, (c + 1) * LANES)
+        first, second, table = first_ref[:, at], second_ref[:, at], table_ref[:, at]
+        first_next = beta_one * first + (1.0 - beta_one) * grad
+        second_next = beta_two * second + (1.0 - beta_two) * grad * grad
+        update = learn_rate * (first_next / corr_one) / (jnp.sqrt(second_next / corr_two) + epsilon)
+        t_out[:, at] = jnp.where(touched, table - update, table)
+        f_out[:, at] = jnp.where(touched, first_next, first)
+        s_out[:, at] = jnp.where(touched, second_next, second)
 
 
 PARAMS = pltpu.CompilerParams(vmem_limit_bytes=32 << 20)
@@ -187,7 +203,7 @@
         scratch_shapes=[
             pltpu.VMEM(grads.shape, jnp.bfloat16),
             pltpu.VMEM(shape, jnp.bfloat16),
-            pltpu.SemaphoreType.DMA((3,)),
+            pltpu.SemaphoreType.DMA((1 + PARTS,)),
         ],
         compiler_params=WIDE,
     )(me, dest, group, row, grads)
@@ -195,7 +211,7 @@
 
 def combine(me, came, groups, rows, cap):
     blocks = (came.shape[1] - TAG_ONE) // cap
-    shape = (groups, blocks * SLOTS + TAG_TWO, LANES)
+    shape = (groups // 2, (blocks + 1) * TILE, LANES)
     return pl.pallas_call(
         functools.partial(combine_kernel, groups, rows, cap),
         out_shape=jax.ShapeDtypeStruct(shape, jnp.bfloat16),
@@ -227,7 +243,9 @@
     packed = pack(at_loc, owner_loc.T, owner_group.T, owner_row.T, token_grads, locs, cap)
     came = lax.all_to_all(packed, "loc", split_axis=0, concat_axis=0, tiled=True)
     sums = combine(at_group, came, groups, rows, cap)
-    landed = lax.all_to_all(sums, "grp", split_axis=0, concat_axis=0, tiled=True)
+    shape = sums.shape
+    sums = sums.reshape(groups, shape[1] // TILE, SLOTS, LANES)
+    landed = lax.all_to_all(sums, "grp", split_axis=0, concat_axis=0, tiled=True).reshape(shape)
     return tuple(update(landed, embed_table, first_moment, second_moment))
 
 

time: 120 us -> 119 us (level)
  blocking collectives: 46.2 us -> 44.8 us
    all_to_all x1, blocking collectives: 46.2 us -> 44.8 us  [per_device(): lax.all_to_all(sums, 'grp', split_axis=0, concat_axis=0, tiled=True)]
where the time goes in v6:
time: 119 us
  waiting for transfers between devices  49.9 us (42%)
  blocking collectives  44.8 us (38%)
  starting transfers between devices  16.8 us (14%)
  Pallas kernels  6.42 us (5%)
    all_to_all x1, waiting for transfers between devices, per_device(): lax.all_to_all(packed, 'loc', split_axis=0, concat_axis=0, tiled=True)  49.9 us
    all_to_all x1, blocking collectives, per_device(): lax.all_to_all(sums, 'grp', split_axis=0, concat_axis=0, tiled=True)  44.8 us
    all_to_all x1, starting transfers between devices, per_device(): lax.all_to_all(packed, 'loc', split_axis=0, concat_axis=0, tiled=True)  16.8 us
    pallas_call x1, Pallas kernels, pack(): pl.pallas_call(functools.partial(pack_kernel, locs, cap), out_shape=jax.S...  3.48 us
  transfers between devices with their start and end apart: 1, of which 1 were waited for; matrix products, arithmetic and copies ran while one was open for 0% of the time, Pallas kernels for 0%

profile of v6, /device:TPU:34, one launch (start us, length us, event | category | flops | bytes accessed | tf_op | source)
XLA Modules:
  0.0 118.6 jit_solution(5306599562489121424)
XLA Ops:
  0.6 3.5 %shard_map.94 = bf16[16,520,128]{2,1,0:T(8,128)(2,1)} custom-call(s32[1]{0:T(128)} %bitcast.1.me_ref, s32[2,128]{1,0:T(2,128)} %bitcast.9, s32[2,128]{1,0:T(2,128)} %bitcast.10, s32[2,128]{1,0:T(2,128)} %bitcast.11, bf16[128,2048]{1,0:T(8,128)(2,1)} %from_ref.1), custom_call_target="tpu_custom_call" | custom-call | tf_op jit(solution)/shard_map/pallas_call | solution.py:198
  4.1 16.8 %all-to-all-start = ((bf16[16,520,128]{2,1,0:T(8,128)(2,1)}), bf16[16,520,128]{2,1,0:T(8,128)(2,1)S(1)}, u32[]{:S(2)}, u32[]{:S(2)}) async-start(bf16[16,520,128]{2,1,0:T(8,128)(2,1)} %shard_map.94), calls=%async_computation | async-start | bytes 4259840 | tf_op jit(solution)/shard_map/all_to_all | solution.py:244
  20.9 49.9 %all-to-all-done.came_ref = bf16[16,520,128]{2,1,0:T(8,128)(2,1)S(1)} async-done(((bf16[16,520,128]{2,1,0:T(8,128)(2,1)}), bf16[16,520,128]{2,1,0:T(8,128)(2,1)S(1)}, u32[]{:S(2)}, u32[]{:S(2)}) %all-to-all-start) | async-done | bytes 2129952 | tf_op jit(solution)/shard_map/all_to_all | solution.py:244
  70.8 0.0 copy-start
  70.8 0.0 copy-start.1
  70.8 0.0 copy-start.2
  70.8 1.5 %shard_map.95 = bf16[32,136,128]{2,1,0:T(8,128)(2,1)S(1)} custom-call(s32[1]{0:T(128)} %bitcast.me_ref, bf16[16,520,128]{2,1,0:T(8,128)(2,1)S(1)} %all-to-all-done.came_ref), custom_call_target="tpu_custom_call" | custom-call | tf_op jit(solution)/shard_map/pallas_call | solution.py:215
  72.3 44.8 %all_to_all.10 = bf16[64,17,4,128]{3,2,1,0:T(4,128)(2,1)S(1)} all-to-all(bf16[64,17,4,128]{3,2,1,0:T(4,128)(2,1)S(1)} %bitcast.8), channel_id=1, replica_groups=mesh['grp'=64,'loc'=16] {'grp'}, dimensions={0} | all-to-all | bytes 2228224 | tf_op jit(solution)/shard_map/all_to_all | solution.py:248
  117.1 0.0 copy-done
  117.1 0.0 copy-done.1
  117.1 0.0 copy-done.2
  117.1 1.5 %shard_map.96 = (f32[32,2048]{1,0:T(8,128)}, f32[32,2048]{1,0:T(8,128)}, f32[32,2048]{1,0:T(8,128)}) custom-call(bf16[32,136,128]{2,1,0:T(8,128)(2,1)S(1)} %bitcast.7, f32[32,2048]{1,0:T(8,128)S(1)} %copy-done, f32[32,2048]{1,0:T(8,128)S(1)} %copy-done.1, f32[32,2048]{1,0:T(8,128)S(1)} %copy-done.2), custom_call_target="tpu_custom_call" | custom-call | tf_op jit(solution)/shard_map/pallas_call | solution.py:225
Async XLA Ops:
  4.1 66.7 %all-to-all-start = ((bf16[16,520,128]{2,1,0:T(8,128)(2,1)}), bf16[16,520,128]{2,1,0:T(8,128)(2,1)S(1)}, u32[]{:S(2)}, u32[]{:S(2)}) async-start(bf16[16,520,128]{2,1,0:T(8,128)(2,1)} %shard_map.94), calls=%async_computation | async-start | bytes 4259840 | tf_op jit(solution)/shard_map/all_to_all | solution.py:244
  70.8 46.3 %copy-start = (f32[32,2048]{1,0:T(8,128)S(1)}, f32[32,2048]{1,0:T(8,128)}, u32[]{:S(2)}) copy-start(f32[32,2048]{1,0:T(8,128)} %table_ref.1) | copy-start | bytes 786436
  70.8 46.3 %copy-start.1 = (f32[32,2048]{1,0:T(8,128)S(1)}, f32[32,2048]{1,0:T(8,128)}, u32[]{:S(2)}) copy-start(f32[32,2048]{1,0:T(8,128)} %first_ref.1) | copy-start | bytes 786436
  70.8 46.3 %copy-start.2 = (f32[32,2048]{1,0:T(8,128)S(1)}, f32[32,2048]{1,0:T(8,128)}, u32[]{:S(2)}) copy-start(f32[32,2048]{1,0:T(8,128)} %second_ref.1) | copy-start | bytes 786436

commit v7 on v6

--- a/solution.py
+++ b/solution.py
@@ -1,4 +1,5 @@
 import functools
+import math
 
 import jax
 import jax.numpy as jnp
@@ -41,7 +42,11 @@
     return lax.dot_general(a, b, NT, preferred_element_type=jnp.float32)
 
 
-def pack_kernel(locs, cap, me_ref, loc_ref, group_ref, row_ref, from_ref, to_ref, grads_ref, out_ref, sem):
+def place_of(group, side):
+    return group // side * 3 % side * side + group % side * 3 % side
+
+
+def pack_kernel(locs, cap, side, me_ref, loc_ref, group_ref, row_ref, from_ref, to_ref, grads_ref, out_ref, sem):
     tokens, width = grads_ref.shape
     read = pltpu.make_async_copy(from_ref, grads_ref, sem.at[0])
     read.start()
@@ -58,7 +63,7 @@
         base += jnp.sum(member, axis=1, keepdims=True)
         rank = jnp.sum(ahead * member, axis=0, keepdims=True).astype(jnp.int32)
         select += jnp.where(dest * cap + rank == iota((locs * cap, tokens), 0), 1.0, 0.0)
-        group = (group_ref[j : j + 1] + 1).astype(jnp.float32)
+        group = (place_of(group_ref[j : j + 1], side) + 1).astype(jnp.float32)
         row = row_ref[j : j + 1].astype(jnp.float32)
         value = jnp.where(kind == 0, group, jnp.where(kind == 1, row, 0.0))
         value = jnp.where(dest == iota((locs * TAG_ONE, tokens), 0) // TAG_ONE, value, 0.0)
@@ -192,11 +197,11 @@
 WIDE = pltpu.CompilerParams(vmem_limit_bytes=60 << 20)
 
 
-def pack(me, dest, group, row, grads, locs, cap):
+def pack(me, dest, group, row, grads, locs, cap, side):
     width = grads.shape[1]
     shape = (locs, width // LANES * cap + TAG_ONE, LANES)
     return pl.pallas_call(
-        functools.partial(pack_kernel, locs, cap),
+        functools.partial(pack_kernel, locs, cap, side),
         out_shape=jax.ShapeDtypeStruct(shape, jnp.bfloat16),
         in_specs=[SMEM, VMEM, VMEM, VMEM, ANY],
         out_specs=ANY,
@@ -239,13 +244,17 @@
     rows = embed_table.shape[0]
     cap = 4 * token_grads.shape[0] // locs
     at_loc = lax.axis_index("loc").astype(jnp.int32).reshape(1)
-    at_group = lax.axis_index("grp").astype(jnp.int32).reshape(1)
-    packed = pack(at_loc, owner_loc.T, owner_group.T, owner_row.T, token_grads, locs, cap)
+    side = math.isqrt(groups)
+    at_group = place_of(lax.axis_index("grp").astype(jnp.int32), side).reshape(1)
+    order = [place_of(g, side) for g in range(groups)]
+    packed = pack(at_loc, owner_loc.T, owner_group.T, owner_row.T, token_grads, locs, cap, side)
     came = lax.all_to_all(packed, "loc", split_axis=0, concat_axis=0, tiled=True)
     sums = combine(at_group, came, groups, rows, cap)
     shape = sums.shape
     sums = sums.reshape(groups, shape[1] // TILE, SLOTS, LANES)
-    landed = lax.all_to_all(sums, "grp", split_axis=0, concat_axis=0, tiled=True).reshape(shape)
+    landed = lax.all_to_all(
+        sums, "grp", split_axis=0, concat_axis=0, tiled=True, axis_index_groups=[order]
+    ).reshape(shape)
     return tuple(update(landed, embed_table, first_moment, second_moment))
 
 

time: 119 us -> 132 us (1.11)
  the two profiles are of different devices: /device:TPU:34 before, /device:TPU:24 now
where the time goes in v7:
time: 132 us
  blocking collectives  57.8 us (44%)
  waiting for transfers between devices  49.8 us (38%)
  starting transfers between devices  16.8 us (13%)
  Pallas kernels  6.43 us (5%)
    all_to_all x1, blocking collectives, per_device(): lax.all_to_all(sums, 'grp', split_axis=0, concat_axis=0, tiled=True, axis...  57.8 us
    all_to_all x1, waiting for transfers between devices, per_device(): lax.all_to_all(packed, 'loc', split_axis=0, concat_axis=0, tiled=True)  49.8 us
    all_to_all x1, starting transfers between devices, per_device(): lax.all_to_all(packed, 'loc', split_axis=0, concat_axis=0, tiled=True)  16.8 us
    pallas_call x1, Pallas kernels, pack(): pl.pallas_call(functools.partial(pack_kernel, locs, cap, side), out_shape...  3.48 us
  transfers between devices with their start and end apart: 1, of which 1 were waited for; matrix products, arithmetic and copies ran while one was open for 0% of the time, Pallas kernels for 0%

profile of v7, /device:TPU:24, one launch (start us, length us, event | category | flops | bytes accessed | tf_op | source)
XLA Modules:
  0.0 131.6 jit_solution(7571528836340139965)
XLA Ops:
  0.6 3.5 %shard_map.94 = bf16[16,520,128]{2,1,0:T(8,128)(2,1)} custom-call(s32[1]{0:T(128)} %bitcast.1.me_ref, s32[2,128]{1,0:T(2,128)} %bitcast.9, s32[2,128]{1,0:T(2,128)} %bitcast.10, s32[2,128]{1,0:T(2,128)} %bitcast.11, bf16[128,2048]{1,0:T(8,128)(2,1)} %from_ref.1), custom_call_target="tpu_custom_call" | custom-call | tf_op jit(solution)/shard_map/pallas_call | solution.py:203
  4.1 16.8 %all-to-all-start = ((bf16[16,520,128]{2,1,0:T(8,128)(2,1)}), bf16[16,520,128]{2,1,0:T(8,128)(2,1)S(1)}, u32[]{:S(2)}, u32[]{:S(2)}) async-start(bf16[16,520,128]{2,1,0:T(8,128)(2,1)} %shard_map.94), calls=%async_computation | async-start | bytes 4259840 | tf_op jit(solution)/shard_map/all_to_all | solution.py:251
  21.0 49.8 %all-to-all-done.came_ref = bf16[16,520,128]{2,1,0:T(8,128)(2,1)S(1)} async-done(((bf16[16,520,128]{2,1,0:T(8,128)(2,1)}), bf16[16,520,128]{2,1,0:T(8,128)(2,1)S(1)}, u32[]{:S(2)}, u32[]{:S(2)}) %all-to-all-start) | async-done | bytes 2129952 | tf_op jit(solution)/shard_map/all_to_all | solution.py:251
  70.8 0.0 copy-start
  70.8 0.0 copy-start.1
  70.8 0.0 copy-start.2
  70.8 1.5 %shard_map.95 = bf16[32,136,128]{2,1,0:T(8,128)(2,1)S(1)} custom-call(s32[1]{0:T(128)} %bitcast.me_ref, bf16[16,520,128]{2,1,0:T(8,128)(2,1)S(1)} %all-to-all-done.came_ref), custom_call_target="tpu_custom_call" | custom-call | tf_op jit(solution)/shard_map/pallas_call | solution.py:220
  72.3 57.8 %all_to_all.10 = bf16[64,17,4,128]{3,2,1,0:T(4,128)(2,1)S(1)} all-to-all(bf16[64,17,4,128]{3,2,1,0:T(4,128)(2,1)S(1)} %bitcast.8), channel_id=1, replica_groups={{0,48,96,16,64,112,32,80,384,432,480,400,448,496,416,464,768,816,864,78..., dimensions={0} | all-to-all | bytes 2228224 | tf_op jit(solution)/shard_map/all_to_all | solution.py:255
  130.1 0.0 copy-done
  130.1 0.0 copy-done.1
  130.1 0.0 copy-done.2
  130.1 1.5 %shard_map.96 = (f32[32,2048]{1,0:T(8,128)}, f32[32,2048]{1,0:T(8,128)}, f32[32,2048]{1,0:T(8,128)}) custom-call(bf16[32,136,128]{2,1,0:T(8,128)(2,1)S(1)} %bitcast.7, f32[32,2048]{1,0:T(8,128)S(1)} %copy-done, f32[32,2048]{1,0:T(8,128)S(1)} %copy-done.1, f32[32,2048]{1,0:T(8,128)S(1)} %copy-done.2), custom_call_target="tpu_custom_call" | custom-call | tf_op jit(solution)/shard_map/pallas_call | solution.py:230
Async XLA Ops:
  4.1 66.7 %all-to-all-start = ((bf16[16,520,128]{2,1,0:T(8,128)(2,1)}), bf16[16,520,128]{2,1,0:T(8,128)(2,1)S(1)}, u32[]{:S(2)}, u32[]{:S(2)}) async-start(bf16[16,520,128]{2,1,0:T(8,128)(2,1)} %shard_map.94), calls=%async_computation | async-start | bytes 4259840 | tf_op jit(solution)/shard_map/all_to_all | solution.py:251
  70.8 59.3 %copy-start = (f32[32,2048]{1,0:T(8,128)S(1)}, f32[32,2048]{1,0:T(8,128)}, u32[]{:S(2)}) copy-start(f32[32,2048]{1,0:T(8,128)} %table_ref.1) | copy-start | bytes 786436
  70.8 59.3 %copy-start.1 = (f32[32,2048]{1,0:T(8,128)S(1)}, f32[32,2048]{1,0:T(8,128)}, u32[]{:S(2)}) copy-start(f32[32,2048]{1,0:T(8,128)} %first_ref.1) | copy-start | bytes 786436
  70.8 59.3 %copy-start.2 = (f32[32,2048]{1,0:T(8,128)S(1)}, f32[32,2048]{1,0:T(8,128)}, u32[]{:S(2)}) copy-start(f32[32,2048]{1,0:T(8,128)} %second_ref.1) | copy-start | bytes 786436

commit v8 on v7

--- a/solution.py
+++ b/solution.py
@@ -42,8 +42,12 @@
     return lax.dot_general(a, b, NT, preferred_element_type=jnp.float32)
 
 
-def place_of(group, side):
-    return group // side * 3 % side * side + group % side * 3 % side
+def group_place(group, side):
+    return group % side * side + group // side
+
+
+def loc_place(loc, locs):
+    return loc % 2 * (locs // 2) + loc // 2
 
 
 def pack_kernel(locs, cap, side, me_ref, loc_ref, group_ref, row_ref, from_ref, to_ref, grads_ref, out_ref, sem):
@@ -57,13 +61,13 @@
     tags = jnp.zeros((locs * TAG_ONE, LANES), jnp.float32)
     kind = iota((locs * TAG_ONE, tokens), 0) % TAG_ONE
     for j in range(2):
-        dest = loc_ref[j : j + 1]
+        dest = loc_place(loc_ref[j : j + 1], locs)
         member = jnp.where(dest == iota((locs, tokens), 0), 1.0, 0.0)
         ahead = dot(member.astype(jnp.bfloat16), before) + base
         base += jnp.sum(member, axis=1, keepdims=True)
         rank = jnp.sum(ahead * member, axis=0, keepdims=True).astype(jnp.int32)
         select += jnp.where(dest * cap + rank == iota((locs * cap, tokens), 0), 1.0, 0.0)
-        group = (place_of(group_ref[j : j + 1], side) + 1).astype(jnp.float32)
+        group = (group_place(group_ref[j : j + 1], side) + 1).astype(jnp.float32)
         row = row_ref[j : j + 1].astype(jnp.float32)
         value = jnp.where(kind == 0, group, jnp.where(kind == 1, row, 0.0))
         value = jnp.where(dest == iota((locs * TAG_ONE, tokens), 0) // TAG_ONE, value, 0.0)
@@ -243,17 +247,20 @@
     groups = lax.axis_size("grp")
     rows = embed_table.shape[0]
     cap = 4 * token_grads.shape[0] // locs
-    at_loc = lax.axis_index("loc").astype(jnp.int32).reshape(1)
+    at_loc = loc_place(lax.axis_index("loc").astype(jnp.int32), locs).reshape(1)
+    loc_order = sorted(range(locs), key=lambda loc: loc_place(loc, locs))
     side = math.isqrt(groups)
-    at_group = place_of(lax.axis_index("grp").astype(jnp.int32), side).reshape(1)
-    order = [place_of(g, side) for g in range(groups)]
+    at_group = group_place(lax.axis_index("grp").astype(jnp.int32), side).reshape(1)
+    group_order = [group_place(g, side) for g in range(groups)]
     packed = pack(at_loc, owner_loc.T, owner_group.T, owner_row.T, token_grads, locs, cap, side)
-    came = lax.all_to_all(packed, "loc", split_axis=0, concat_axis=0, tiled=True)
+    came = lax.all_to_all(
+        packed, "loc", split_axis=0, concat_axis=0, tiled=True, axis_index_groups=[loc_order]
+    )
     sums = combine(at_group, came, groups, rows, cap)
     shape = sums.shape
     sums = sums.reshape(groups, shape[1] // TILE, SLOTS, LANES)
     landed = lax.all_to_all(
-        sums, "grp", split_axis=0, concat_axis=0, tiled=True, axis_index_groups=[order]
+        sums, "grp", split_axis=0, concat_axis=0, tiled=True, axis_index_groups=[group_order]
     ).reshape(shape)
     return tuple(update(landed, embed_table, first_moment, second_moment))
 

time: 132 us -> 118 us (0.89)
  the two profiles are of different devices: /device:TPU:24 before, /device:TPU:4 now
where the time goes in v8:
time: 118 us
  waiting for transfers between devices  48.8 us (41%)
  blocking collectives  45.4 us (38%)
  starting transfers between devices  16.8 us (14%)
  Pallas kernels  6.43 us (5%)
    all_to_all x1, waiting for transfers between devices, per_device(): lax.all_to_all(packed, 'loc', split_axis=0, concat_axis=0, tiled=True, ax...  48.8 us
    all_to_all x1, blocking collectives, per_device(): lax.all_to_all(sums, 'grp', split_axis=0, concat_axis=0, tiled=True, axis...  45.4 us
    all_to_all x1, starting transfers between devices, per_device(): lax.all_to_all(packed, 'loc', split_axis=0, concat_axis=0, tiled=True, ax...  16.8 us
    pallas_call x1, Pallas kernels, pack(): pl.pallas_call(functools.partial(pack_kernel, locs, cap, side), out_shape...  3.48 us
  transfers between devices with their start and end apart: 1, of which 1 were waited for; matrix products, arithmetic and copies ran while one was open for 0% of the time, Pallas kernels for 0%

profile of v8, /device:TPU:4, one launch (start us, length us, event | category | flops | bytes accessed | tf_op | source)
XLA Modules:
  0.0 118.2 jit_solution(16157128900424836124)
XLA Ops:
  0.7 3.5 %shard_map.94 = bf16[16,520,128]{2,1,0:T(8,128)(2,1)} custom-call(s32[1]{0:T(128)} %bitcast.1.me_ref, s32[2,128]{1,0:T(2,128)} %bitcast.9, s32[2,128]{1,0:T(2,128)} %bitcast.10, s32[2,128]{1,0:T(2,128)} %bitcast.11, bf16[128,2048]{1,0:T(8,128)(2,1)} %from_ref.1), custom_call_target="tpu_custom_call" | custom-call | tf_op jit(solution)/shard_map/pallas_call | solution.py:207
  4.1 16.8 %all-to-all-start = ((bf16[16,520,128]{2,1,0:T(8,128)(2,1)}), bf16[16,520,128]{2,1,0:T(8,128)(2,1)S(1)}, u32[]{:S(2)}, u32[]{:S(2)}) async-start(bf16[16,520,128]{2,1,0:T(8,128)(2,1)} %shard_map.94), calls=%async_computation | async-start | bytes 4259840 | tf_op jit(solution)/shard_map/all_to_all | solution.py:256
  21.0 48.8 %all-to-all-done.came_ref = bf16[16,520,128]{2,1,0:T(8,128)(2,1)S(1)} async-done(((bf16[16,520,128]{2,1,0:T(8,128)(2,1)}), bf16[16,520,128]{2,1,0:T(8,128)(2,1)S(1)}, u32[]{:S(2)}, u32[]{:S(2)}) %all-to-all-start) | async-done | bytes 2129952 | tf_op jit(solution)/shard_map/all_to_all | solution.py:256
  69.8 0.0 copy-start
  69.8 0.0 copy-start.1
  69.8 0.0 copy-start.2
  69.8 1.5 %shard_map.95 = bf16[32,136,128]{2,1,0:T(8,128)(2,1)S(1)} custom-call(s32[1]{0:T(128)} %bitcast.me_ref, bf16[16,520,128]{2,1,0:T(8,128)(2,1)S(1)} %all-to-all-done.came_ref), custom_call_target="tpu_custom_call" | custom-call | tf_op jit(solution)/shard_map/pallas_call | solution.py:224
  71.2 45.4 %all_to_all.10 = bf16[64,17,4,128]{3,2,1,0:T(4,128)(2,1)S(1)} all-to-all(bf16[64,17,4,128]{3,2,1,0:T(4,128)(2,1)S(1)} %bitcast.8), channel_id=1, replica_groups={{0,128,256,384,512,640,768,896,16,144,272,400,528,656,784,912,32,160,28..., dimensions={0} | all-to-all | bytes 2228224 | tf_op jit(solution)/shard_map/all_to_all | solution.py:262
  116.7 0.0 copy-done
  116.7 0.0 copy-done.1
  116.7 0.0 copy-done.2
  116.7 1.5 %shard_map.96 = (f32[32,2048]{1,0:T(8,128)}, f32[32,2048]{1,0:T(8,128)}, f32[32,2048]{1,0:T(8,128)}) custom-call(bf16[32,136,128]{2,1,0:T(8,128)(2,1)S(1)} %bitcast.7, f32[32,2048]{1,0:T(8,128)S(1)} %copy-done, f32[32,2048]{1,0:T(8,128)S(1)} %copy-done.1, f32[32,2048]{1,0:T(8,128)S(1)} %copy-done.2), custom_call_target="tpu_custom_call" | custom-call | tf_op jit(solution)/shard_map/pallas_call | solution.py:234
Async XLA Ops:
  4.1 65.6 %all-to-all-start = ((bf16[16,520,128]{2,1,0:T(8,128)(2,1)}), bf16[16,520,128]{2,1,0:T(8,128)(2,1)S(1)}, u32[]{:S(2)}, u32[]{:S(2)}) async-start(bf16[16,520,128]{2,1,0:T(8,128)(2,1)} %shard_map.94), calls=%async_computation | async-start | bytes 4259840 | tf_op jit(solution)/shard_map/all_to_all | solution.py:256
  69.8 46.9 %copy-start = (f32[32,2048]{1,0:T(8,128)S(1)}, f32[32,2048]{1,0:T(8,128)}, u32[]{:S(2)}) copy-start(f32[32,2048]{1,0:T(8,128)} %table_ref.1) | copy-start | bytes 786436
  69.8 46.9 %copy-start.1 = (f32[32,2048]{1,0:T(8,128)S(1)}, f32[32,2048]{1,0:T(8,128)}, u32[]{:S(2)}) copy-start(f32[32,2048]{1,0:T(8,128)} %first_ref.1) | copy-start | bytes 786436
  69.8 46.9 %copy-start.2 = (f32[32,2048]{1,0:T(8,128)S(1)}, f32[32,2048]{1,0:T(8,128)}, u32[]{:S(2)}) copy-start(f32[32,2048]{1,0:T(8,128)} %second_ref.1) | copy-start | bytes 786436

commit v9 on v8

--- a/solution.py
+++ b/solution.py
@@ -43,7 +43,7 @@
 
 
 def group_place(group, side):
-    return group % side * side + group // side
+    return (group // side - group % side + side) % side * side + group % side
 
 
 def loc_place(loc, locs):
@@ -251,7 +251,7 @@
     loc_order = sorted(range(locs), key=lambda loc: loc_place(loc, locs))
     side = math.isqrt(groups)
     at_group = group_place(lax.axis_index("grp").astype(jnp.int32), side).reshape(1)
-    group_order = [group_place(g, side) for g in range(groups)]
+    group_order = sorted(range(groups), key=lambda group: group_place(group, side))
     packed = pack(at_loc, owner_loc.T, owner_group.T, owner_row.T, token_grads, locs, cap, side)
     came = lax.all_to_all(
         packed, "loc", split_axis=0, concat_axis=0, tiled=True, axis_index_groups=[loc_order]

time: 118 us -> 118 us (level)
  the two profiles are of different devices: /device:TPU:4 before, /device:TPU:2 now
where the time goes in v9:
time: 118 us
  waiting for transfers between devices  48.8 us (41%)
  blocking collectives  45.1 us (38%)
  starting transfers between devices  16.8 us (14%)
  Pallas kernels  6.43 us (5%)
    all_to_all x1, waiting for transfers between devices, per_device(): lax.all_to_all(packed, 'loc', split_axis=0, concat_axis=0, tiled=True, ax...  48.8 us
    all_to_all x1, blocking collectives, per_device(): lax.all_to_all(sums, 'grp', split_axis=0, concat_axis=0, tiled=True, axis...  45.1 us
    all_to_all x1, starting transfers between devices, per_device(): lax.all_to_all(packed, 'loc', split_axis=0, concat_axis=0, tiled=True, ax...  16.8 us
    pallas_call x1, Pallas kernels, pack(): pl.pallas_call(functools.partial(pack_kernel, locs, cap, side), out_shape...  3.48 us
  transfers between devices with their start and end apart: 1, of which 1 were waited for; matrix products, arithmetic and copies ran while one was open for 0% of the time, Pallas kernels for 0%

profile of v9, /device:TPU:2, one launch (start us, length us, event | category | flops | bytes accessed | tf_op | source)
XLA Modules:
  0.0 117.9 jit_solution(16322726424093586265)
XLA Ops:
  0.7 3.5 %shard_map.94 = bf16[16,520,128]{2,1,0:T(8,128)(2,1)} custom-call(s32[1]{0:T(128)} %bitcast.1.me_ref, s32[2,128]{1,0:T(2,128)} %bitcast.9, s32[2,128]{1,0:T(2,128)} %bitcast.10, s32[2,128]{1,0:T(2,128)} %bitcast.11, bf16[128,2048]{1,0:T(8,128)(2,1)} %from_ref.1), custom_call_target="tpu_custom_call" | custom-call | tf_op jit(solution)/shard_map/pallas_call | solution.py:207
  4.1 16.8 %all-to-all-start = ((bf16[16,520,128]{2,1,0:T(8,128)(2,1)}), bf16[16,520,128]{2,1,0:T(8,128)(2,1)S(1)}, u32[]{:S(2)}, u32[]{:S(2)}) async-start(bf16[16,520,128]{2,1,0:T(8,128)(2,1)} %shard_map.94), calls=%async_computation | async-start | bytes 4259840 | tf_op jit(solution)/shard_map/all_to_all | solution.py:256
  21.0 48.8 %all-to-all-done.came_ref = bf16[16,520,128]{2,1,0:T(8,128)(2,1)S(1)} async-done(((bf16[16,520,128]{2,1,0:T(8,128)(2,1)}), bf16[16,520,128]{2,1,0:T(8,128)(2,1)S(1)}, u32[]{:S(2)}, u32[]{:S(2)}) %all-to-all-start) | async-done | bytes 2129952 | tf_op jit(solution)/shard_map/all_to_all | solution.py:256
  69.8 0.0 copy-start
  69.8 0.0 copy-start.1
  69.8 0.0 copy-start.2
  69.8 1.5 %shard_map.95 = bf16[32,136,128]{2,1,0:T(8,128)(2,1)S(1)} custom-call(s32[1]{0:T(128)} %bitcast.me_ref, bf16[16,520,128]{2,1,0:T(8,128)(2,1)S(1)} %all-to-all-done.came_ref), custom_call_target="tpu_custom_call" | custom-call | tf_op jit(solution)/shard_map/pallas_call | solution.py:224
  71.2 45.1 %all_to_all.10 = bf16[64,17,4,128]{3,2,1,0:T(4,128)(2,1)S(1)} all-to-all(bf16[64,17,4,128]{3,2,1,0:T(4,128)(2,1)S(1)} %bitcast.8), channel_id=1, replica_groups={{0,144,288,432,576,720,864,1008,128,272,416,560,704,848,992,112,256,400..., dimensions={0} | all-to-all | bytes 2228224 | tf_op jit(solution)/shard_map/all_to_all | solution.py:262
  116.4 0.0 copy-done
  116.4 0.0 copy-done.1
  116.4 0.0 copy-done.2
  116.4 1.5 %shard_map.96 = (f32[32,2048]{1,0:T(8,128)}, f32[32,2048]{1,0:T(8,128)}, f32[32,2048]{1,0:T(8,128)}) custom-call(bf16[32,136,128]{2,1,0:T(8,128)(2,1)S(1)} %bitcast.7, f32[32,2048]{1,0:T(8,128)S(1)} %copy-done, f32[32,2048]{1,0:T(8,128)S(1)} %copy-done.1, f32[32,2048]{1,0:T(8,128)S(1)} %copy-done.2), custom_call_target="tpu_custom_call" | custom-call | tf_op jit(solution)/shard_map/pallas_call | solution.py:234
Async XLA Ops:
  4.1 65.6 %all-to-all-start = ((bf16[16,520,128]{2,1,0:T(8,128)(2,1)}), bf16[16,520,128]{2,1,0:T(8,128)(2,1)S(1)}, u32[]{:S(2)}, u32[]{:S(2)}) async-start(bf16[16,520,128]{2,1,0:T(8,128)(2,1)} %shard_map.94), calls=%async_computation | async-start | bytes 4259840 | tf_op jit(solution)/shard_map/all_to_all | solution.py:256
  69.8 46.6 %copy-start = (f32[32,2048]{1,0:T(8,128)S(1)}, f32[32,2048]{1,0:T(8,128)}, u32[]{:S(2)}) copy-start(f32[32,2048]{1,0:T(8,128)} %table_ref.1) | copy-start | bytes 786436
  69.8 46.6 %copy-start.1 = (f32[32,2048]{1,0:T(8,128)S(1)}, f32[32,2048]{1,0:T(8,128)}, u32[]{:S(2)}) copy-start(f32[32,2048]{1,0:T(8,128)} %first_ref.1) | copy-start | bytes 786436
  69.8 46.6 %copy-start.2 = (f32[32,2048]{1,0:T(8,128)S(1)}, f32[32,2048]{1,0:T(8,128)}, u32[]{:S(2)}) copy-start(f32[32,2048]{1,0:T(8,128)} %second_ref.1) | copy-start | bytes 786436

commit v10 on v8

--- a/solution.py
+++ b/solution.py
@@ -50,10 +50,15 @@
     return loc % 2 * (locs // 2) + loc // 2
 
 
-def pack_kernel(locs, cap, side, me_ref, loc_ref, group_ref, row_ref, from_ref, to_ref, grads_ref, out_ref, sem):
+def pack_kernel(locs, cap, side, me_ref, loc_from, group_from, row_from, from_ref, to_ref, *scratch):
+    loc_ref, group_ref, row_ref, grads_ref, out_ref, sem = scratch
+    sources = (loc_from, group_from, row_from, from_ref)
+    reads = [pltpu.make_async_copy(a, b, sem.at[i]) for i, (a, b) in enumerate(zip(sources, scratch))]
+    for read in reads:
+        read.start()
     tokens, width = grads_ref.shape
-    read = pltpu.make_async_copy(from_ref, grads_ref, sem.at[0])
-    read.start()
+    for read in reads[:3]:
+        read.wait()
     shift = me_ref[0] % (LANES // cap) * cap
     before = ones(iota((tokens, tokens), 0) < iota((tokens, tokens), 1))
     base = jnp.zeros((locs, 1), jnp.float32)
@@ -75,7 +80,7 @@
     select = select.astype(jnp.bfloat16)
     blocks = width // LANES
     out_ref[:, blocks * cap :, :] = tags.reshape(locs, TAG_ONE, LANES).astype(jnp.bfloat16)
-    read.wait()
+    reads[3].wait()
     half = locs // PARTS
     writes = []
     for h in range(PARTS):
@@ -87,7 +92,7 @@
                 piece = part[:, i * LANES : (i + 1) * LANES].reshape(half, cap, LANES)
                 out_ref[dests, (c + i) * cap : (c + i + 1) * cap, :] = piece
         at = pl.ds(h * half, half)
-        writes.append(pltpu.make_async_copy(out_ref.at[at], to_ref.at[at], sem.at[1 + h]))
+        writes.append(pltpu.make_async_copy(out_ref.at[at], to_ref.at[at], sem.at[len(reads) + h]))
         writes[-1].start()
     for write in writes:
         write.wait()
@@ -152,7 +157,7 @@
     out_ref[:, blocks * TILE :, :] = tile(up(sums[blocks - 1]), mark).astype(jnp.bfloat16)
 
 
-def update_kernel(landed_ref, table_ref, first_ref, second_ref, t_out, f_out, s_out):
+def update_kernel(landed_ref, table_ref, first_ref, second_ref, t_to, f_to, s_to, t_out, f_out, s_out, sem):
     pairs = landed_ref.shape[0]
     rows, width = table_ref.shape
     blocks = width // LANES
@@ -185,6 +190,7 @@
     halves.append(dot(members[1][:rows], end.astype(jnp.bfloat16)))
     corr_one = 1.0 - beta_one**ADAM_STEP
     corr_two = 1.0 - beta_two**ADAM_STEP
+    writes = []
     for c in range(blocks):
         grad = halves[c] + halves[blocks + 1 + c]
         at = slice(c * LANES, (c + 1) * LANES)
@@ -195,6 +201,13 @@
         t_out[:, at] = jnp.where(touched, table - update, table)
         f_out[:, at] = jnp.where(touched, first_next, first)
         s_out[:, at] = jnp.where(touched, second_next, second)
+        if (c + 1) % (blocks // 2) == 0:
+            done = pl.ds((c + 1 - blocks // 2) * LANES, blocks // 2 * LANES)
+            for a, b in ((t_out, t_to), (f_out, f_to), (s_out, s_to)):
+                writes.append(pltpu.make_async_copy(a.at[:, done], b.at[:, done], sem.at[len(writes)]))
+                writes[-1].start()
+    for write in writes:
+        write.wait()
 
 
 PARAMS = pltpu.CompilerParams(vmem_limit_bytes=32 << 20)
@@ -207,12 +220,15 @@
     return pl.pallas_call(
         functools.partial(pack_kernel, locs, cap, side),
         out_shape=jax.ShapeDtypeStruct(shape, jnp.bfloat16),
-        in_specs=[SMEM, VMEM, VMEM, VMEM, ANY],
+        in_specs=[SMEM, ANY, ANY, ANY, ANY],
         out_specs=ANY,
         scratch_shapes=[
+            pltpu.VMEM(dest.shape, jnp.int32),
+            pltpu.VMEM(group.shape, jnp.int32),
+            pltpu.VMEM(row.shape, jnp.int32),
             pltpu.VMEM(grads.shape, jnp.bfloat16),
             pltpu.VMEM(shape, jnp.bfloat16),
-            pltpu.SemaphoreType.DMA((1 + PARTS,)),
+            pltpu.SemaphoreType.DMA((4 + PARTS,)),
         ],
         compiler_params=WIDE,
     )(me, dest, group, row, grads)
@@ -235,7 +251,8 @@
         update_kernel,
         out_shape=(jax.ShapeDtypeStruct(table.shape, table.dtype),) * 3,
         in_specs=[VMEM] * 4,
-        out_specs=(VMEM,) * 3,
+        out_specs=(ANY,) * 3,
+        scratch_shapes=[pltpu.VMEM(table.shape, table.dtype)] * 3 + [pltpu.SemaphoreType.DMA((6,))],
         compiler_params=PARAMS,
     )(landed, table, first, second)
 

time: 118 us -> 118 us (level)
  no operation moved by 1% of the time
where the time goes in v10:
time: 118 us
  waiting for transfers between devices  48.8 us (41%)
  blocking collectives  45.4 us (38%)
  starting transfers between devices  16.8 us (14%)
  Pallas kernels  5.91 us (5%)
    all_to_all x1, waiting for transfers between devices, per_device(): lax.all_to_all(packed, 'loc', split_axis=0, concat_axis=0, tiled=True, ax...  48.8 us
    all_to_all x1, blocking collectives, per_device(): lax.all_to_all(sums, 'grp', split_axis=0, concat_axis=0, tiled=True, axis...  45.4 us
    all_to_all x1, starting transfers between devices, per_device(): lax.all_to_all(packed, 'loc', split_axis=0, concat_axis=0, tiled=True, ax...  16.8 us
    pallas_call x1, Pallas kernels, pack(): pl.pallas_call(functools.partial(pack_kernel, locs, cap, side), out_shape...  2.91 us
  transfers between devices with their start and end apart: 1, of which 1 were waited for; matrix products, arithmetic and copies ran while one was open for 0% of the time, Pallas kernels for 0%

profile of v10, /device:TPU:4, one launch (start us, length us, event | category | flops | bytes accessed | tf_op | source)
XLA Modules:
  0.0 117.7 jit_solution(7843317176150981636)
XLA Ops:
  0.7 2.9 %shard_map.94 = bf16[16,520,128]{2,1,0:T(8,128)(2,1)} custom-call(s32[1]{0:T(128)} %bitcast.1.me_ref, s32[2,128]{1,0:T(2,128)} %bitcast.9, s32[2,128]{1,0:T(2,128)} %bitcast.10, s32[2,128]{1,0:T(2,128)} %bitcast.11, bf16[128,2048]{1,0:T(8,128)(2,1)} %from_ref.1), custom_call_target="tpu_custom_call" | custom-call | tf_op jit(solution)/shard_map/pallas_call | solution.py:220
  3.6 16.8 %all-to-all-start = ((bf16[16,520,128]{2,1,0:T(8,128)(2,1)}), bf16[16,520,128]{2,1,0:T(8,128)(2,1)S(1)}, u32[]{:S(2)}, u32[]{:S(2)}) async-start(bf16[16,520,128]{2,1,0:T(8,128)(2,1)} %shard_map.94), calls=%async_computation | async-start | bytes 4259840 | tf_op jit(solution)/shard_map/all_to_all | solution.py:273
  20.4 48.8 %all-to-all-done.came_ref = bf16[16,520,128]{2,1,0:T(8,128)(2,1)S(1)} async-done(((bf16[16,520,128]{2,1,0:T(8,128)(2,1)}), bf16[16,520,128]{2,1,0:T(8,128)(2,1)S(1)}, u32[]{:S(2)}, u32[]{:S(2)}) %all-to-all-start) | async-done | bytes 2129952 | tf_op jit(solution)/shard_map/all_to_all | solution.py:273
  69.2 0.0 copy-start
  69.2 0.0 copy-start.1
  69.2 0.0 copy-start.2
  69.2 1.5 %shard_map.95 = bf16[32,136,128]{2,1,0:T(8,128)(2,1)S(1)} custom-call(s32[1]{0:T(128)} %bitcast.me_ref, bf16[16,520,128]{2,1,0:T(8,128)(2,1)S(1)} %all-to-all-done.came_ref), custom_call_target="tpu_custom_call" | custom-call | tf_op jit(solution)/shard_map/pallas_call | solution.py:240
  70.7 45.4 %all_to_all.10 = bf16[64,17,4,128]{3,2,1,0:T(4,128)(2,1)S(1)} all-to-all(bf16[64,17,4,128]{3,2,1,0:T(4,128)(2,1)S(1)} %bitcast.8), channel_id=1, replica_groups={{0,128,256,384,512,640,768,896,16,144,272,400,528,656,784,912,32,160,28..., dimensions={0} | all-to-all | bytes 2228224 | tf_op jit(solution)/shard_map/all_to_all | solution.py:279
  116.1 0.0 copy-done
  116.1 0.0 copy-done.1
  116.1 0.0 copy-done.2
  116.1 1.5 %shard_map.96 = (f32[32,2048]{1,0:T(8,128)}, f32[32,2048]{1,0:T(8,128)}, f32[32,2048]{1,0:T(8,128)}) custom-call(bf16[32,136,128]{2,1,0:T(8,128)(2,1)S(1)} %bitcast.7, f32[32,2048]{1,0:T(8,128)S(1)} %copy-done, f32[32,2048]{1,0:T(8,128)S(1)} %copy-done.1, f32[32,2048]{1,0:T(8,128)S(1)} %copy-done.2), custom_call_target="tpu_custom_call" | custom-call | tf_op jit(solution)/shard_map/pallas_call | solution.py:250
Async XLA Ops:
  3.6 65.6 %all-to-all-start = ((bf16[16,520,128]{2,1,0:T(8,128)(2,1)}), bf16[16,520,128]{2,1,0:T(8,128)(2,1)S(1)}, u32[]{:S(2)}, u32[]{:S(2)}) async-start(bf16[16,520,128]{2,1,0:T(8,128)(2,1)} %shard_map.94), calls=%async_computation | async-start | bytes 4259840 | tf_op jit(solution)/shard_map/all_to_all | solution.py:273
  69.2 46.9 %copy-start = (f32[32,2048]{1,0:T(8,128)S(1)}, f32[32,2048]{1,0:T(8,128)}, u32[]{:S(2)}) copy-start(f32[32,2048]{1,0:T(8,128)} %table_ref.1) | copy-start | bytes 786436
  69.2 46.9 %copy-start.1 = (f32[32,2048]{1,0:T(8,128)S(1)}, f32[32,2048]{1,0:T(8,128)}, u32[]{:S(2)}) copy-start(f32[32,2048]{1,0:T(8,128)} %first_ref.1) | copy-start | bytes 786436
  69.2 46.9 %copy-start.2 = (f32[32,2048]{1,0:T(8,128)S(1)}, f32[32,2048]{1,0:T(8,128)}, u32[]{:S(2)}) copy-start(f32[32,2048]{1,0:T(8,128)} %second_ref.1) | copy-start | bytes 786436
